TPU v7x, 512 devices: a whole 4x4x16 slice. The times are simulated.
512 devices in a mesh: island: 8 (over x_lo, y), fsdp: 64 (over z, x_hi, core).
Axes of the slice: x: 4 (x_hi: 2, x_lo: 2; x = x_hi * 2 + x_lo), y: 4, z: 16, core: 2. Of those that a mesh axis runs over, the one named last changes fastest.
Arguments:
- activations: bfloat16 [131072, 8192], P(('island', 'fsdp')), may hold values from -24 to 24
- cotangent: bfloat16 [131072, 128], P(('island', 'fsdp')), may hold values from -0.0625 to 0.0625
- norm_gain: float32 [8, 8192], P('island'), may hold values from 0.5 to 1.5
- weight: bfloat16 [8, 8192, 128], P('island', 'fsdp'), may hold values from -0.0625 to 0.0625
- global_slab: float32 [64, 28672], P(None, 'fsdp'), may hold values from -6 to 6
- local_slab: bfloat16 [8, 64, 28672], P('island', None, 'fsdp'), may hold values from -6 to 6
- momentum: float32 [64, 28672], P(None, 'fsdp'), may hold values from -6 to 6
Outputs:
- values: bfloat16 [131072, 128], P(('island', 'fsdp'))
- weight_grad: float32 [8, 8192, 128], P('island', 'fsdp')
- gain_grad: float32 [8, 8192], P('island')
- new_global: float32 [64, 28672], P(None, 'fsdp')
- new_momentum: float32 [64, 28672], P(None, 'fsdp')
All inputs are finite; a program needn't handle non-finite values.
Results may differ from a plain program's by a relative error of at most 0.02.
Values may be sent and summed in bfloat16 or wider, within the bound.
No kernel may reach another device: no remote copies, remote signals or barrier semaphores. Data moves between devices by JAX's collectives and lax.ppermute only.
A program may use at most 64 MiB of HBM per device.

v0:
```python
import jax
import jax.numpy as jnp
from jax import lax
from jax.sharding import PartitionSpec as P


def outer_update(average, params, moment):
    new_moment = 0.9 * moment + average
    return (params - 0.7 * (average + 0.9 * new_moment), new_moment)


def shards(activations, cotangent, norm_gain, weight, global_slab, local_slab, momentum):
    tokens = activations.astype(jnp.float32)
    inverse = lax.rsqrt(jnp.mean(tokens * tokens, axis=1, keepdims=True) + 1e-05)
    unit = tokens * inverse
    normed = (unit * norm_gain).astype(jnp.bfloat16)
    shard = weight[0]
    columns = normed
    projected = jnp.dot(
        columns,
        lax.all_gather(shard, "fsdp", axis=0, tiled=True),
        preferred_element_type=jnp.float32,
    )
    partial_grad = lax.dot_general(
        cotangent,
        lax.all_gather(shard, "fsdp", axis=0, tiled=True),
        (((1,), (1,)), ((), ())),
        preferred_element_type=jnp.float32,
    )
    columns = unit
    gain_part = jnp.sum(partial_grad * columns, axis=0, keepdims=True)
    gain_grad = lax.psum(gain_part, "fsdp")
    columns = normed
    weight_grad = lax.psum_scatter(
        lax.dot_general(
            columns, cotangent, (((0,), (0,)), ((), ())), preferred_element_type=jnp.float32
        ),
        "fsdp",
        scatter_dimension=0,
        tiled=True,
    )
    delta = global_slab - local_slab[0].astype(jnp.float32)
    replicas = lax.axis_size("island")
    summed = lax.psum(delta.astype(jnp.bfloat16), "island").astype(jnp.float32)
    new_global, new_momentum = outer_update(summed / replicas, global_slab, momentum)
    return (projected.astype(jnp.bfloat16), weight_grad[None], gain_grad, new_global, new_momentum)


def solution(mesh):
    placed = (
        P(("island", "fsdp"), None),
        P(("island", "fsdp"), None),
        P("island", None),
        P("island", "fsdp", None),
        P(None, "fsdp"),
        P("island", None, "fsdp"),
        P(None, "fsdp"),
    )
    return jax.shard_map(
        shards,
        mesh=mesh,
        in_specs=placed,
        out_specs=(
            P(("island", "fsdp"), None),
            P("island", "fsdp", None),
            P("island", None),
            P(None, "fsdp"),
            P(None, "fsdp"),
        ),
        check_vma=False,
    )
```

profile of v0, /device:TPU:1, one launch (start us, length us, event | category | flops | bytes accessed | tf_op | source)
XLA Modules:
  0.0 428.1 jit_solution(9227251894807400312)
XLA Ops:
  7.2 0.0 copy-start
  7.2 0.0 copy-start.4
  7.2 0.0 all-gather.3.cloned.1.call-start
  7.2 0.7 all-gather.3.cloned.1.call-update
  7.9 0.0 reduce-scatter.2.cloned.1.call-start
  8.0 0.0 copy-start.1
  8.0 3.3 fusion.2
  11.2 0.0 copy-done
  11.3 0.0 copy-done.4
  11.3 0.2 copy-done.1
  11.4 3.7 fusion.7
  15.2 0.0 copy-start.2
  15.2 0.0 copy-start.5
  15.2 0.0 copy-start.3
  15.2 0.0 reduce-scatter.2.cloned.1.call-update
  15.2 0.9 copy-done.2
  16.1 0.0 copy-done.5
  16.1 28.5 %psum.15 = bf16[64,448]{1,0:T(8,128)(2,1)S(1)} all-reduce(bf16[64,448]{1,0:T(8,128)(2,1)S(1)} %fusion.15), channel_id=1, replica_groups=mesh['island'=8,'fsdp'=64] {'island'}, use_global_device_ids=true, to_apply=%region_4.0 | all-reduce | flops 28672 | bytes 114688 | tf_op jit(solution)/shard_map/psum | solution.py:44
  44.6 0.0 copy-done.3
  44.6 0.7 multiply_subtract_fusion
  45.4 115.5 %all-gather.3.cloned.1.call-done = bf16[1,8192,128]{2,1,0:T(8,128)(2,1)} async-done(((bf16[1,128,128]{2,1,0:T(8,128)(2,1)}), bf16[1,8192,128]{2,1,0:T(8,128)(2,1)}) %all-gather.3.cloned.1.call-update) | async-done | bytes 2097168 | tf_op jit(solution)/shard_map/all_gather | solution.py:21
  160.8 0.0 copy-start.6
  160.8 4.3 fusion.3
  165.1 251.8 %psum.14 = f32[1,8192]{1,0:T(1,128)} all-reduce(f32[1,8192]{1,0:T(1,128)S(1)} %bitcast.17), channel_id=1, replica_groups=mesh['island'=8,'fsdp'=64] {'fsdp'}, use_global_device_ids=true, to_apply=%region_3.0 | all-reduce | flops 8192 | bytes 65536 | tf_op jit(solution)/shard_map/psum | solution.py:32
  417.0 0.0 copy-done.6
  417.0 4.3 fusion.10
  421.2 0.0 reduce-scatter.2.cloned.1.call-done
  (2 shorter events, 0.0 us)
Async XLA Ops:
  7.2 4.1 copy-start
  7.2 4.1 copy-start.4
  7.2 153.7 %all-gather.3.cloned.1.call-start = ((), (), s32[]{:S(2)}) async-start(), calls=%async_computation.2 | async-start | bytes 2129920 | tf_op jit(solution)/shard_map/all_gather | solution.py:21
  7.9 413.3 %reduce-scatter.2.cloned.1.call-start = ((), (), s32[]{:S(2)}) async-start(), calls=%async_computation.1 | async-start | bytes 4259840 | tf_op jit(solution)/shard_map/reduce_scatter | solution.py:34
  8.0 3.5 copy-start.1
  15.2 0.9 copy-start.2
  15.2 0.9 copy-start.5
  15.2 29.5 %copy-start.3 = (f32[64,448]{1,0:T(8,128)S(1)}, f32[64,448]{1,0:T(8,128)}, u32[]{:S(2)}) copy-start(f32[64,448]{1,0:T(8,128)} %param.13) | copy-start | bytes 344068
  160.8 256.1 %copy-start.6 = (bf16[1,8192,128]{2,1,0:T(8,128)(2,1)S(1)}, bf16[1,8192,128]{2,1,0:T(8,128)(2,1)}, u32[]{:S(2)}) copy-start(bf16[1,8192,128]{2,1,0:T(8,128)(2,1)} %all-gather.3.cloned.1.call-done) | copy-start | bytes 6291460
Sparse Core Ops, SparseCore 0:
  11.3 149.4 all-gather.2
  166.1 206.3 reduce-scatter.1
where the time goes:
time: 433 us; the launch traced here: 428 us
  blocking collectives  280 us (65%)
  waiting for transfers between devices  116 us (27%)
  between operations  14.1 us (3%)
  matrix products  12.3 us (3%)
    psum x1, blocking collectives, shards(): gain_grad = lax.psum(gain_part, 'fsdp')  252 us
    all_gather x1, waiting for transfers between devices, shards(): lax.all_gather(shard, 'fsdp', axis=0, tiled=True)  115 us
    psum x1, blocking collectives, shards(): summed = lax.psum(delta.astype(jnp.bfloat16), 'island').astype(jnp.float32)  28.5 us
  transfers between devices with their start and end apart: 2, of which 1 were waited for; matrix products, arithmetic and copies ran while one was open for 4% of the time, Pallas kernels for 0%

commit v1 on v0

v1 whole, which is shorter than its diff:
```python
import jax
import jax.numpy as jnp
import numpy as np
from jax import lax
from jax.sharding import Mesh, PartitionSpec as P

Z, XH, CORE = 16, 2, 2
FSDP = ("z", "xh", "core")
f32, bf16 = jnp.float32, jnp.bfloat16


def swap(value, axis):
    return lax.ppermute(value, axis, [(0, 1), (1, 0)])


def to_all(value, axis, size):
    return lax.all_to_all(jnp.broadcast_to(value[None], (size,) + value.shape), axis, 0, 0)


def pair(mine, other, index, axis):
    first = jnp.where(index == 0, mine, other)
    second = jnp.where(index == 0, other, mine)
    return jnp.stack([first, second], axis=axis)


def shards(activations, cotangent, norm_gain, weight, global_slab, local_slab, momentum):
    xh, core = lax.axis_index("xh"), lax.axis_index("core")
    own = lambda a, i, axis: lax.dynamic_index_in_dim(a, i, axis, keepdims=False)
    gain = norm_gain.reshape(Z, XH, CORE, 128)
    gain_class = own(own(gain, core, 2), xh, 1)

    with jax.named_scope("weight_over_z"):
        weight_z = to_all(weight[0], "z", Z)

    with jax.named_scope("projection_grad"):
        tokens = activations.astype(f32)
        inverse = lax.rsqrt(jnp.mean(tokens * tokens, axis=1, keepdims=True) + 1e-05)
        scaled = (cotangent.astype(f32) * inverse).astype(bf16)
        grad = lax.dot_general(
            activations, scaled, (((0,), (0,)), ((), ())), preferred_element_type=f32
        ).astype(bf16)
        grad = grad.reshape(Z, XH, CORE, 128, 128)
        there = swap(own(grad, 1 - core, 2), "core")
        grad = own(grad, core, 2).astype(f32) + there.astype(f32)
        there = swap(own(grad, 1 - xh, 1).astype(bf16), "xh")
        grad = own(grad, xh, 1) + there.astype(f32)
        grad_own = jnp.sum(lax.all_to_all(grad.astype(bf16), "z", 0, 0).astype(f32), axis=0)

    with jax.named_scope("gain_grad"):
        part = jnp.sum(weight_z.astype(f32) * grad, axis=-1)
        part = jnp.sum(to_all(part, "z", Z), axis=0)
        gain_grad = to_all(part, ("xh", "core"), XH * CORE)
        gain_grad = gain_grad.reshape(XH, CORE, Z, 128).transpose(2, 0, 1, 3)

    with jax.named_scope("values"):
        scaled_weight = (weight_z.astype(f32) * gain_class[:, :, None]).astype(bf16)
        scaled_weight = pair(scaled_weight, swap(scaled_weight, "xh"), xh, 1)
        scaled_weight = pair(scaled_weight, swap(scaled_weight, "core"), core, 2)
        values = jnp.dot(
            activations, scaled_weight.reshape(8192, 128), preferred_element_type=f32
        )
        values = (values * inverse).astype(bf16)

    with jax.named_scope("outer_update"):
        delta = (global_slab - local_slab[0].astype(f32)).astype(bf16)
        average = jnp.sum(to_all(delta, "island", 8).astype(f32), axis=0) / 8
        new_momentum = 0.9 * momentum + average
        new_global = global_slab - 0.7 * (average + 0.9 * new_momentum)

    fsdp_index = (lax.axis_index("z") * XH + xh) * CORE + core
    gain_own = lax.dynamic_index_in_dim(norm_gain.reshape(64, 128), fsdp_index, 0, False)
    weight_grad = grad_own * gain_own[:, None]
    return (values, weight_grad[None], gain_grad.reshape(1, 8192), new_global, new_momentum)


def solution(mesh):
    mesh = Mesh(np.asarray(mesh.devices).reshape(8, Z, XH, CORE), ("island",) + FSDP)
    every = ("island",) + FSDP
    placed = (
        P(every, None),
        P(every, None),
        P("island", None),
        P("island", FSDP, None),
        P(None, FSDP),
        P("island", None, FSDP),
        P(None, FSDP),
    )
    return jax.shard_map(
        shards,
        mesh=mesh,
        in_specs=placed,
        out_specs=(
            P(every, None),
            P("island", FSDP, None),
            P("island", None),
            P(None, FSDP),
            P(None, FSDP),
        ),
        check_vma=False,
    )
```

time: 433 us -> 157 us (0.36)
  the two profiles are of different devices: /device:TPU:1 before, /device:TPU:2 now
where the time goes in v1:
time: 157 us; the launch traced here: 156 us
  waiting for transfers between devices  64.6 us (41%)
  starting transfers between devices  50.7 us (32%)
  local copies, waits for them, and re-layouts  25.1 us (16%)
  other arithmetic  10.4 us (7%)
  matrix products  4.54 us (3%)
    all_to_all x4, starting transfers between devices, to_all(): lax.all_to_all(jnp.broadcast_to(value[None], (size,) + value.shape), axis...  31.4 us
    all_to_all x4, waiting for transfers between devices, to_all(): lax.all_to_all(jnp.broadcast_to(value[None], (size,) + value.shape), axis...  31.4 us
    all_to_all x1, waiting for transfers between devices, shards(): lax.all_to_all(grad.astype(bf16), 'z', 0, 0).astype(f32)  18.6 us
    ppermute x4, waiting for transfers between devices, swap(): return lax.ppermute(value, axis, [(0, 1), (1, 0)])  14.7 us
    ppermute x4, starting transfers between devices, swap(): return lax.ppermute(value, axis, [(0, 1), (1, 0)])  11.9 us
    unnamed x19, local copies, waits for them, and re-layouts  10.8 us
    all_to_all x1, starting transfers between devices, shards(): lax.all_to_all(grad.astype(bf16), 'z', 0, 0).astype(f32)  7.43 us
    dynamic_slice x2, local copies, waits for them, and re-layouts, shards(): lax.dynamic_index_in_dim(a, i, axis, keepdims=False)  7.31 us
  transfers between devices with their start and end apart: 9, of which 7 were waited for; matrix products, arithmetic and copies ran while one was open for 7% of the time, Pallas kernels for 0%

profile of v1, /device:TPU:2, one launch (start us, length us, event | category | flops | bytes accessed | tf_op | source)
XLA Modules:
  0.0 156.4 jit_solution(9233972049939051643)
XLA Ops:
  0.7 3.3 %multiply_reduce_fusion = f32[256]{0:T(256)S(1)} fusion(bf16[256,8192]{1,0:T(8,128)(2,1)} %param.7), kind=kLoop, calls=%fused_computation.2 | loop fusion | flops 6291200 | bytes 4195328 | tf_op jit(solution)/shard_map/projection_grad/reduce_sum | solution.py:37
  4.1 3.0 %fusion = bf16[8192,128]{0,1:T(8,128)(2,1)} fusion(bf16[256,8192]{1,0:T(8,128)(2,1)S(1)} %copy-done.1, bf16[256,128]{1,0:T(8,128)(2,1)} %param.8, f32[256]{0:T(256)S(1)} %add_rsqrt_fusion), kind=kOutput, calls=%fused_computation.1 | convolution fusion | flops 538017792 | bytes 6358016 | tf_op jit(solution)/shard_map/projection_grad/dot_general | solution.py:39
  7.1 3.2 %reshape.83 = bf16[16,2,2,128,128]{3,2,1,0,4:T(2,128)(2,1)S(1)} reshape(bf16[8192,128]{0,1:T(8,128)(2,1)} %fusion) | data formatting | bytes 4194304 | tf_op jit(solution)/shard_map/projection_grad/reshape | solution.py:42
  10.3 7.3 %constant_dynamic-slice_fusion.2 = (bf16[16,2,1,128,128]{3,2,1,0,4:T(2,128)(2,1)}, bf16[16,2,1,128,128]{3,2,1,0,4:T(2,128)(2,1)}) fusion(bf16[16,2,2,128,128]{3,2,1,0,4:T(2,128)(2,1)S(1)} %reshape.83, s32[]{:T(128)S(6)} %select_n.54, s32[]{:T(128)S(6)} %select_n.60), kind=kLoop, calls=%fused_computation.32 | loop fusion | bytes 4194312 | tf_op jit(solution)/shard_map/projection_grad/jit(dynamic_index_in_dim)/dynamic_slice | solution.py:28
  17.6 6.0 %copy.32 = bf16[16,2,1,128,128]{4,3,1,0,2:T(8,128)(2,1)} copy(bf16[16,2,1,128,128]{3,2,1,0,4:T(2,128)(2,1)} %get-tuple-element.30) | data formatting | bytes 2097152
  23.7 1.9 %collective-permute-start.2 = (bf16[16,2,128,128]{3,2,1,0:T(8,128)(2,1)}, bf16[16,2,128,128]{3,2,1,0:T(8,128)(2,1)}, u32[]{:S(2)}, u32[]{:S(2)}) collective-permute-start(bf16[16,2,128,128]{3,2,1,0:T(8,128)(2,1)} %bitcast.13), channel_id=1, source_target_pairs={{0,1},{1,0},{2,3},{3,2},{4,5},{5,4},{6,7},{7,6},{8,9},{9,8},{10,11... | collective-permute-start | bytes 3145736 | tf_op jit(solution)/shard_map/projection_grad/ppermute | solution.py:13
  25.6 0.9 broadcast_in_dim.11
  26.5 15.2 %all-to-all-start = ((bf16[16,128,128]{2,1,0:T(8,128)(2,1)}), bf16[16,128,128]{2,1,0:T(8,128)(2,1)}, u32[]{:S(2)}, u32[]{:S(2)}) async-start(bf16[16,128,128]{2,1,0:T(8,128)(2,1)} %broadcast_in_dim.11), calls=%async_computation | async-start | bytes 1048576 | tf_op jit(solution)/shard_map/weight_over_z/all_to_all | solution.py:17
  41.8 1.9 %copy.31 = bf16[16,2,1,128,128]{4,3,1,0,2:T(8,128)(2,1)S(1)} copy(bf16[16,2,1,128,128]{3,2,1,0,4:T(2,128)(2,1)S(1)} %copy-done.3) | data formatting | bytes 2097152
  43.7 1.6 %convert_add_fusion = f32[16,2,128,128]{3,2,1,0:T(8,128)S(1)} fusion(bf16[16,2,128,128]{3,2,1,0:T(8,128)(2,1)} %collective-permute-done.2, bf16[16,2,1,128,128]{4,3,1,0,2:T(8,128)(2,1)S(1)} %copy.31), kind=kLoop, calls=%fused_computation.4 | loop fusion | flops 1572864 | bytes 4194304 | tf_op jit(solution)/shard_map/projection_grad/add | solution.py:44
  45.4 4.0 %collective-permute-start.3 = (bf16[16,128,128]{2,1,0:T(8,128)(2,1)S(1)}, bf16[16,128,128]{2,1,0:T(8,128)(2,1)S(1)}, u32[]{:S(2)}, u32[]{:S(2)}) collective-permute-start(bf16[16,128,128]{2,1,0:T(8,128)(2,1)S(1)} %fusion.6), channel_id=1, source_target_pairs={{0,2},{2,0},{1,3},{3,1},{4,6},{6,4},{5,7},{7,5},{8,10},{10,8},{9,1... | collective-permute-start | bytes 1572872 | tf_op jit(solution)/shard_map/projection_grad/ppermute | solution.py:13
  49.5 13.4 %collective-permute-done.3 = bf16[16,128,128]{2,1,0:T(8,128)(2,1)S(1)} collective-permute-done((bf16[16,128,128]{2,1,0:T(8,128)(2,1)S(1)}, bf16[16,128,128]{2,1,0:T(8,128)(2,1)S(1)}, u32[]{:S(2)}, u32[]{:S(2)}) %collective-permute-start.3) | collective-permute-done | bytes 524320 | tf_op jit(solution)/shard_map/projection_grad/ppermute | solution.py:13
  62.8 8.2 %all-to-all-done = bf16[16,128,128]{2,1,0:T(8,128)(2,1)} async-done(((bf16[16,128,128]{2,1,0:T(8,128)(2,1)}), bf16[16,128,128]{2,1,0:T(8,128)(2,1)}, u32[]{:S(2)}, u32[]{:S(2)}) %all-to-all-start) | async-done | bytes 524320 | tf_op jit(solution)/shard_map/weight_over_z/all_to_all | solution.py:17
  71.0 2.4 %fusion.4 = (f32[16,128]{1,0:T(8,128)S(1)}, bf16[16,128,128]{2,1,0:T(8,128)(2,1)}, bf16[16,128,128]{2,1,0:T(8,128)(2,1)S(1)}) fusion(bf16[16,128,128]{2,1,0:T(8,128)(2,1)} %all-to-all-done, bf16[16,128,128]{2,1,0:T(8,128)(2,1)S(1)} %collective-permute-done.3, f32[16,2,128,128]{3,2,1,0:T(8,128)S(1)} %convert_add_fusion, s32[]{:T(128)S(6)} %select_n.52, ...), kind=kLoop, calls=%fused_computation.11 | loop fusion | flops 2095104 | bytes 3162116 | tf_op jit(solution)/shard_map/gain_grad/reduce_sum | solution.py:50
  74.1 6.9 %all-to-all-start.2 = ((f32[16,16,128]{2,1,0:T(8,128)}), f32[16,16,128]{2,1,0:T(8,128)S(1)}, u32[]{:S(2)}, u32[]{:S(2)}) async-start(f32[16,16,128]{2,1,0:T(8,128)} %broadcast_in_dim.12), calls=%async_computation.2 | async-start | bytes 262144 | tf_op jit(solution)/shard_map/gain_grad/all_to_all | solution.py:17
  81.0 4.0 %collective-permute-start = (bf16[16,128,128]{2,1,0:T(8,128)(2,1)S(1)}, bf16[16,128,128]{2,1,0:T(8,128)(2,1)S(1)}, u32[]{:S(2)}, u32[]{:S(2)}) collective-permute-start(bf16[16,128,128]{2,1,0:T(8,128)(2,1)S(1)} %get-tuple-element.35), channel_id=1, source_target_pairs={{0,2},{2,0},{1,3},{3,1},{4,6},{6,4},{5,7},{7,5},{8,10},{10,8},{9,1... | collective-permute-start | bytes 1572872 | tf_op jit(solution)/shard_map/values/ppermute | solution.py:13
  85.1 10.6 %all-to-all-done.2 = f32[16,16,128]{2,1,0:T(8,128)S(1)} async-done(((f32[16,16,128]{2,1,0:T(8,128)}), f32[16,16,128]{2,1,0:T(8,128)S(1)}, u32[]{:S(2)}, u32[]{:S(2)}) %all-to-all-start.2) | async-done | bytes 131104 | tf_op jit(solution)/shard_map/gain_grad/all_to_all | solution.py:17
  95.6 0.8 broadcast_in_dim.14
  96.5 5.9 %all-to-all-start.4 = ((bf16[8,64,448]{2,1,0:T(8,128)(2,1)}), bf16[8,64,448]{2,1,0:T(8,128)(2,1)S(1)}, u32[]{:S(2)}, u32[]{:S(2)}) async-start(bf16[8,64,448]{2,1,0:T(8,128)(2,1)} %broadcast_in_dim.14), calls=%async_computation.4 | async-start | bytes 1048576 | tf_op jit(solution)/shard_map/outer_update/all_to_all | solution.py:17
  102.5 7.2 %all-to-all-done.4 = bf16[8,64,448]{2,1,0:T(8,128)(2,1)S(1)} async-done(((bf16[8,64,448]{2,1,0:T(8,128)(2,1)}), bf16[8,64,448]{2,1,0:T(8,128)(2,1)S(1)}, u32[]{:S(2)}, u32[]{:S(2)}) %all-to-all-start.4) | async-done | bytes 458784 | tf_op jit(solution)/shard_map/outer_update/all_to_all | solution.py:17
  110.3 3.4 %all-to-all-start.3 = ((f32[4,16,128]{2,1,0:T(8,128)}), f32[4,16,128]{2,1,0:T(8,128)S(1)}, u32[]{:S(2)}, u32[]{:S(2)}) async-start(f32[4,16,128]{2,1,0:T(8,128)} %broadcast_in_dim.13), calls=%async_computation.3 | async-start | bytes 65536 | tf_op jit(solution)/shard_map/gain_grad/all_to_all | solution.py:17
  113.8 5.4 %all-to-all-done.3 = f32[4,16,128]{2,1,0:T(8,128)S(1)} async-done(((f32[4,16,128]{2,1,0:T(8,128)}), f32[4,16,128]{2,1,0:T(8,128)S(1)}, u32[]{:S(2)}, u32[]{:S(2)}) %all-to-all-start.3) | async-done | bytes 32800 | tf_op jit(solution)/shard_map/gain_grad/all_to_all | solution.py:17
  119.1 7.4 %all-to-all-start.1 = ((bf16[16,128,128]{2,1,0:T(8,128)(2,1)}), bf16[16,128,128]{2,1,0:T(8,128)(2,1)S(1)}, u32[]{:S(2)}, u32[]{:S(2)}) async-start(bf16[16,128,128]{2,1,0:T(8,128)(2,1)} %get-tuple-element.28), calls=%async_computation.1 | async-start | bytes 1048576 | tf_op jit(solution)/shard_map/projection_grad/all_to_all | solution.py:47
  126.6 1.1 pad_maximum_fusion.1
  127.6 1.9 %collective-permute-start.1 = (bf16[16,2,128,128]{3,2,1,0:T(8,128)(2,1)}, bf16[16,2,128,128]{3,2,1,0:T(8,128)(2,1)S(1)}, u32[]{:S(2)}, u32[]{:S(2)}) collective-permute-start(bf16[16,2,128,128]{3,2,1,0:T(8,128)(2,1)} %pad_maximum_fusion.1), channel_id=1, source_target_pairs={{0,1},{1,0},{2,3},{3,2},{4,5},{5,4},{6,7},{7,6},{8,9},{9,8},{10,11... | collective-permute-start | bytes 3145736 | tf_op jit(solution)/shard_map/values/ppermute | solution.py:13
  129.7 0.7 multiply_subtract_fusion
  131.0 1.3 collective-permute-done.1
  132.8 2.0 %copy-done.2 = bf16[256,8192]{1,0:T(8,128)(2,1)S(1)} copy-done((bf16[256,8192]{1,0:T(8,128)(2,1)S(1)}, bf16[256,8192]{1,0:T(8,128)(2,1)}, u32[]{:S(2)}) %copy-start.2) | copy-done | bytes 4194328
  134.7 1.5 fusion.2
  136.3 0.7 copy.30
  137.0 18.6 %all-to-all-done.1 = bf16[16,128,128]{2,1,0:T(8,128)(2,1)S(1)} async-done(((bf16[16,128,128]{2,1,0:T(8,128)(2,1)}), bf16[16,128,128]{2,1,0:T(8,128)(2,1)S(1)}, u32[]{:S(2)}, u32[]{:S(2)}) %all-to-all-start.1) | async-done | bytes 524320 | tf_op jit(solution)/shard_map/projection_grad/all_to_all | solution.py:47
  155.6 0.7 bitcast_multiply_fusion
  (31 shorter events, 2.9 us)
Async XLA Ops:
  0.6 48.8 %copy-start = (f32[1,8192]{1,0:T(1,128)S(1)}, f32[1,8192]{1,0:T(1,128)}, u32[]{:S(2)}) copy-start(f32[1,8192]{1,0:T(1,128)} %param.9) | copy-start | bytes 98308
  0.7 3.5 %copy-start.1 = (bf16[256,8192]{1,0:T(8,128)(2,1)S(1)}, bf16[256,8192]{1,0:T(8,128)(2,1)}, u32[]{:S(2)}) copy-start(bf16[256,8192]{1,0:T(8,128)(2,1)} %param.7) | copy-start | bytes 12582916
  17.6 8.0 %copy-start.7 = (bf16[1,128,128]{2,1,0:T(8,128)(2,1)S(1)}, bf16[1,128,128]{2,1,0:T(8,128)(2,1)}, u32[]{:S(2)}) copy-start(bf16[1,128,128]{2,1,0:T(8,128)(2,1)} %param.10) | copy-start | bytes 98308
  17.6 24.1 %copy-start.3 = (bf16[16,2,1,128,128]{3,2,1,0,4:T(2,128)(2,1)S(1)}, bf16[16,2,1,128,128]{3,2,1,0,4:T(2,128)(2,1)}, u32[]{:S(2)}) copy-start(bf16[16,2,1,128,128]{3,2,1,0,4:T(2,128)(2,1)} %get-tuple-element.29) | copy-start | bytes 3145732
  23.7 20.0 %collective-permute-start.2 = (bf16[16,2,128,128]{3,2,1,0:T(8,128)(2,1)}, bf16[16,2,128,128]{3,2,1,0:T(8,128)(2,1)}, u32[]{:S(2)}, u32[]{:S(2)}) collective-permute-start(bf16[16,2,128,128]{3,2,1,0:T(8,128)(2,1)} %bitcast.13), channel_id=1, source_target_pairs={{0,1},{1,0},{2,3},{3,2},{4,5},{5,4},{6,7},{7,6},{8,9},{9,8},{10,11... | collective-permute-start | bytes 3145736 | tf_op jit(solution)/shard_map/projection_grad/ppermute | solution.py:13
  26.5 44.5 %all-to-all-start = ((bf16[16,128,128]{2,1,0:T(8,128)(2,1)}), bf16[16,128,128]{2,1,0:T(8,128)(2,1)}, u32[]{:S(2)}, u32[]{:S(2)}) async-start(bf16[16,128,128]{2,1,0:T(8,128)(2,1)} %broadcast_in_dim.11), calls=%async_computation | async-start | bytes 1048576 | tf_op jit(solution)/shard_map/weight_over_z/all_to_all | solution.py:17
  45.2 39.8 %copy-start.4 = (f32[64,448]{1,0:T(8,128)S(1)}, f32[64,448]{1,0:T(8,128)}, u32[]{:S(2)}) copy-start(f32[64,448]{1,0:T(8,128)} %param.11) | copy-start | bytes 344068
  45.2 39.8 %copy-start.6 = (bf16[1,64,448]{2,1,0:T(8,128)(2,1)S(1)}, bf16[1,64,448]{2,1,0:T(8,128)(2,1)}, u32[]{:S(2)}) copy-start(bf16[1,64,448]{2,1,0:T(8,128)(2,1)} %param.12) | copy-start | bytes 172036
  45.4 17.4 %collective-permute-start.3 = (bf16[16,128,128]{2,1,0:T(8,128)(2,1)S(1)}, bf16[16,128,128]{2,1,0:T(8,128)(2,1)S(1)}, u32[]{:S(2)}, u32[]{:S(2)}) collective-permute-start(bf16[16,128,128]{2,1,0:T(8,128)(2,1)S(1)} %fusion.6), channel_id=1, source_target_pairs={{0,2},{2,0},{1,3},{3,1},{4,6},{6,4},{5,7},{7,5},{8,10},{10,8},{9,1... | collective-permute-start | bytes 1572872 | tf_op jit(solution)/shard_map/projection_grad/ppermute | solution.py:13
  74.1 21.5 %all-to-all-start.2 = ((f32[16,16,128]{2,1,0:T(8,128)}), f32[16,16,128]{2,1,0:T(8,128)S(1)}, u32[]{:S(2)}, u32[]{:S(2)}) async-start(f32[16,16,128]{2,1,0:T(8,128)} %broadcast_in_dim.12), calls=%async_computation.2 | async-start | bytes 262144 | tf_op jit(solution)/shard_map/gain_grad/all_to_all | solution.py:17
  81.0 32.7 %collective-permute-start = (bf16[16,128,128]{2,1,0:T(8,128)(2,1)S(1)}, bf16[16,128,128]{2,1,0:T(8,128)(2,1)S(1)}, u32[]{:S(2)}, u32[]{:S(2)}) collective-permute-start(bf16[16,128,128]{2,1,0:T(8,128)(2,1)S(1)} %get-tuple-element.35), channel_id=1, source_target_pairs={{0,2},{2,0},{1,3},{3,1},{4,6},{6,4},{5,7},{7,5},{8,10},{10,8},{9,1... | collective-permute-start | bytes 1572872 | tf_op jit(solution)/shard_map/values/ppermute | solution.py:13
  96.5 13.2 %all-to-all-start.4 = ((bf16[8,64,448]{2,1,0:T(8,128)(2,1)}), bf16[8,64,448]{2,1,0:T(8,128)(2,1)S(1)}, u32[]{:S(2)}, u32[]{:S(2)}) async-start(bf16[8,64,448]{2,1,0:T(8,128)(2,1)} %broadcast_in_dim.14), calls=%async_computation.4 | async-start | bytes 1048576 | tf_op jit(solution)/shard_map/outer_update/all_to_all | solution.py:17
  110.3 8.8 %all-to-all-start.3 = ((f32[4,16,128]{2,1,0:T(8,128)}), f32[4,16,128]{2,1,0:T(8,128)S(1)}, u32[]{:S(2)}, u32[]{:S(2)}) async-start(f32[4,16,128]{2,1,0:T(8,128)} %broadcast_in_dim.13), calls=%async_computation.3 | async-start | bytes 65536 | tf_op jit(solution)/shard_map/gain_grad/all_to_all | solution.py:17
  113.8 15.9 %copy-start.5 = (f32[64,448]{1,0:T(8,128)S(1)}, f32[64,448]{1,0:T(8,128)}, u32[]{:S(2)}) copy-start(f32[64,448]{1,0:T(8,128)} %param.13) | copy-start | bytes 344068
  119.1 36.4 %all-to-all-start.1 = ((bf16[16,128,128]{2,1,0:T(8,128)(2,1)}), bf16[16,128,128]{2,1,0:T(8,128)(2,1)S(1)}, u32[]{:S(2)}, u32[]{:S(2)}) async-start(bf16[16,128,128]{2,1,0:T(8,128)(2,1)} %get-tuple-element.28), calls=%async_computation.1 | async-start | bytes 1048576 | tf_op jit(solution)/shard_map/projection_grad/all_to_all | solution.py:47
  127.6 4.8 %collective-permute-start.1 = (bf16[16,2,128,128]{3,2,1,0:T(8,128)(2,1)}, bf16[16,2,128,128]{3,2,1,0:T(8,128)(2,1)S(1)}, u32[]{:S(2)}, u32[]{:S(2)}) collective-permute-start(bf16[16,2,128,128]{3,2,1,0:T(8,128)(2,1)} %pad_maximum_fusion.1), channel_id=1, source_target_pairs={{0,1},{1,0},{2,3},{3,2},{4,5},{5,4},{6,7},{7,6},{8,9},{9,8},{10,11... | collective-permute-start | bytes 3145736 | tf_op jit(solution)/shard_map/values/ppermute | solution.py:13
  132.5 2.2 %copy-start.2 = (bf16[256,8192]{1,0:T(8,128)(2,1)S(1)}, bf16[256,8192]{1,0:T(8,128)(2,1)}, u32[]{:S(2)}) copy-start(bf16[256,8192]{1,0:T(8,128)(2,1)} %param.7) | copy-start | bytes 12582916

commit v2 on v1

v2 whole, which is shorter than its diff:
```python
import functools

import jax
import jax.numpy as jnp
import numpy as np
from jax import lax
from jax.experimental import pallas as pl
from jax.experimental.pallas import tpu as pltpu
from jax.sharding import Mesh, PartitionSpec as P

FSDP = ("zh", "zl", "xh", "core")
QUAD = ("zl", "xh")
ZL = XH = CORE = 2
B = 128
f32, bf16 = jnp.float32, jnp.bfloat16
SMEM = pl.BlockSpec(memory_space=pltpu.SMEM)
VMEM = pl.BlockSpec(memory_space=pltpu.VMEM)
LIMIT = 60 * 2**20
SMALL = 20 * 2**20


def swap(value, axis, flip=1, size=2):
    return lax.ppermute(value, axis, [(i, i ^ flip) for i in range(size)])


def to_all(value, axis, size):
    return lax.all_to_all(jnp.broadcast_to(value[None], (size,) + value.shape), axis, 0, 0)


def whole(*shape):
    return pl.BlockSpec(shape, lambda *_: (0,) * len(shape))


def project_kernel(rows, place, x, cot, keep, send, inverse, scaled):
    tokens, width = x.shape
    for i in range(0, tokens, rows):
        total = jnp.zeros((rows, B), f32)
        for c in range(0, width, B):
            block = x[pl.ds(i, rows), pl.ds(c, B)].astype(f32)
            total += block * block
        mean = jnp.sum(total, axis=1, keepdims=True) * (1 / width)
        unit = lax.rsqrt(mean + 1e-05)
        inverse[pl.ds(i, rows), :] = unit
        scaled[pl.ds(i, rows), :] = cot[pl.ds(i, rows), :].astype(f32) * unit
    left = scaled[...].T.astype(bf16)
    core = place[0]
    for k in range(width // (CORE * B)):
        both = jnp.dot(left, x[:, pl.ds(k * CORE * B, CORE * B)], preferred_element_type=f32)
        both = both.astype(bf16)
        first, second = both[:, :B], both[:, B:]
        at, z = k % (ZL * XH), k // (ZL * XH)
        keep[at, z] = jnp.where(core == 0, first, second)
        send[at, z] = jnp.where(core == 0, second, first)


def project(place, activations, cotangent):
    tokens, width = activations.shape
    rows = 32
    half = jax.ShapeDtypeStruct((ZL * XH, width // (ZL * XH * CORE * B), B, B), bf16)
    return pl.pallas_call(
        functools.partial(project_kernel, rows),
        out_shape=(half, half, jax.ShapeDtypeStruct((tokens, 1), f32)),
        in_specs=[SMEM, VMEM, VMEM],
        out_specs=[VMEM] * 3,
        scratch_shapes=[
            pltpu.VMEM((tokens, B), f32),
        ],
        compiler_params=pltpu.CompilerParams(vmem_limit_bytes=SMALL),
        cost_estimate=pl.CostEstimate(
            flops=2 * tokens * width * B, bytes_accessed=3 * tokens * width, transcendentals=0
        ),
        name="project",
    )(place, activations, cotangent)


def relative(i, quad):
    low, high = quad % 2, quad // 2
    return (1 - high if i // 2 else high) * 2 + (1 - low if i % 2 else low)


def merge_kernel(place, keep, core_part, one, two, three, own):
    for i, out in enumerate((own, one, two, three)):
        at = relative(i, place[1])
        for z in range(keep.shape[1]):
            total = keep[at, z].astype(f32) + core_part[at, z].astype(f32)
            out[z] = total.astype(out.dtype)


def merge(place, keep, core_part):
    quad, z = keep.shape[:2]
    block = jax.ShapeDtypeStruct((z, B, B), bf16)
    return pl.pallas_call(
        merge_kernel,
        grid=(1,),
        out_shape=(block,) * 3 + (jax.ShapeDtypeStruct((z, B, B), f32),),
        in_specs=[SMEM] + [whole(*keep.shape)] * 2,
        out_specs=[whole(z, B, B)] * 4,
        compiler_params=pltpu.CompilerParams(vmem_limit_bytes=SMALL),
        cost_estimate=pl.CostEstimate(
            flops=quad * z * B * B, bytes_accessed=7 * quad * z * B * B, transcendentals=0
        ),
        name="merge",
    )(place, keep, core_part)


def combine_kernel(place, own, one, two, three, weight, out, gain):
    depth = own.shape[0]
    zl = place[1] // XH
    for z in range(depth):
        total = own[z] + one[z].astype(f32) + two[z].astype(f32) + three[z].astype(f32)
        out[z, pl.ds(0, B), :] = total.astype(bf16)
        terms = total * weight[ZL * z + zl].astype(f32).T
        gain[pl.ds(z, 1), :] = jnp.sum(terms, axis=0, keepdims=True)
    high = gain[...].astype(bf16)
    low = (gain[...] - high.astype(f32)).astype(bf16)
    terms = jnp.concatenate([high.astype(f32), low.astype(f32)], axis=0).astype(bf16)
    for z in range(depth):
        out[z, pl.ds(B, 2 * depth), :] = terms


def combine(place, own, parts, weight):
    z = own.shape[0]
    return pl.pallas_call(
        combine_kernel,
        grid=(1,),
        out_shape=jax.ShapeDtypeStruct((z, B + 2 * z, B), bf16),
        in_specs=[SMEM] + [whole(z, B, B)] * 4 + [whole(ZL * z, B, B)],
        out_specs=whole(z, B + 2 * z, B),
        scratch_shapes=[pltpu.VMEM((z, B), f32)],
        compiler_params=pltpu.CompilerParams(vmem_limit_bytes=SMALL),
        cost_estimate=pl.CostEstimate(
            flops=6 * z * B * B, bytes_accessed=14 * z * B * B, transcendentals=0
        ),
        name="combine",
    )(place, own, *parts, weight)


def values_kernel(place, x, inverse, gain, w00, w01, w10, w11, out):
    core = place[0]
    same = place[1] % XH == 0
    column = gain[...].T
    total = jnp.zeros(out.shape, f32)
    for k in range(x.shape[1] // (CORE * B)):
        xh, z = k % XH, k // XH
        near = same if xh == 0 else jnp.logical_not(same)
        here = jnp.where(near, w00[z].astype(f32), w01[z].astype(f32))
        there = jnp.where(near, w10[z].astype(f32), w11[z].astype(f32))
        first = jnp.where(core == 0, here, there) * column[:, 2 * k : 2 * k + 1]
        second = jnp.where(core == 0, there, here) * column[:, 2 * k + 1 : 2 * k + 2]
        weight = jnp.concatenate([first, second], axis=0).astype(bf16)
        columns = pl.ds(k * CORE * B, CORE * B)
        total += jnp.dot(x[:, columns], weight, preferred_element_type=f32)
    out[...] = (total * inverse[...]).astype(bf16)


def project_forward(place, activations, inverse, gain, pieces):
    tokens, width = activations.shape
    return pl.pallas_call(
        values_kernel,
        out_shape=jax.ShapeDtypeStruct((tokens, B), bf16),
        in_specs=[SMEM] + [VMEM] * 7,
        out_specs=VMEM,
        compiler_params=pltpu.CompilerParams(vmem_limit_bytes=SMALL),
        cost_estimate=pl.CostEstimate(
            flops=2 * tokens * width * B, bytes_accessed=3 * tokens * width, transcendentals=0
        ),
        name="project_forward",
    )(place, activations, inverse, gain.reshape(-1, B), *pieces)


def sum_over_islands(delta, islands, flips):
    for flip in [f for f in flips if f < islands]:
        delta = delta + swap(delta, "island", flip, islands)
    return delta


def shards(activations, cotangent, norm_gain, weight, global_slab, local_slab, momentum):
    quad, core = lax.axis_index(QUAD), lax.axis_index("core")
    depth, islands = lax.axis_size("zh"), lax.axis_size("island")
    place = jnp.stack([core, quad]).astype(jnp.int32)

    with jax.named_scope("weight_over_z"):
        weight_z = to_all(weight[0], ("zh", "zl"), depth * ZL)

    with jax.named_scope("projection_grad"):
        keep, send, inverse = project(place, activations, cotangent)
        core_part = swap(send, "core")
        *sent, own = merge(place, keep, core_part)
        parts = [swap(part, QUAD, i, 4) for i, part in zip((1, 2, 3), sent)]

    with jax.named_scope("average_over_islands"):
        local, own = lax.optimization_barrier((local_slab, own))
        delta = (global_slab - local[0].astype(f32)).astype(bf16)
        average = sum_over_islands(delta.astype(f32), islands, (1, 3))

    with jax.named_scope("projection_grad"):
        combined = combine(place, own, parts, weight_z)
        combined, average = lax.optimization_barrier((combined, average))
        chunks = lax.all_to_all(combined, "zh", 0, 0)

    with jax.named_scope("values"):
        w01 = swap(weight_z, "xh")
        pieces = (weight_z, w01, swap(weight_z, "core"), swap(w01, "core"))
        values = project_forward(place, activations, inverse, norm_gain, pieces)

    with jax.named_scope("gain_grad"):
        chunks, *rest = lax.optimization_barrier((chunks, pieces[2], pieces[3]))
        gain_grad = jnp.sum(chunks[:, B:].astype(f32), axis=0)
        gain_grad = gain_grad[:depth] + gain_grad[depth:]
        gain_grad = to_all(gain_grad, QUAD + ("core",), ZL * XH * CORE)
        gain_grad = gain_grad.transpose(1, 0, 2)

    with jax.named_scope("weight_grad"):
        row = (lax.axis_index("zh") * ZL * XH + quad) * CORE + core
        gain_own = lax.dynamic_index_in_dim(norm_gain.reshape(-1, B), row, 0, True)
        weight_grad = (jnp.sum(chunks[:, :B].astype(f32), axis=0) * gain_own).T

    with jax.named_scope("outer_update"):
        average = sum_over_islands(average, islands, (4,)) / islands
        new_momentum = 0.9 * momentum + average
        new_global = global_slab - 0.7 * (average + 0.9 * new_momentum)

    return (values, weight_grad[None], gain_grad.reshape(1, -1), new_global, new_momentum)


def solution(mesh):
    islands, fsdp = mesh.shape["island"], mesh.shape["fsdp"]
    grid = np.asarray(mesh.devices).reshape(islands, fsdp // (ZL * XH * CORE), ZL, XH, CORE)
    every = ("island",) + FSDP
    return jax.shard_map(
        shards,
        mesh=Mesh(grid, every),
        in_specs=(
            P(every, None),
            P(every, None),
            P("island", None),
            P("island", FSDP, None),
            P(None, FSDP),
            P("island", None, FSDP),
            P(None, FSDP),
        ),
        out_specs=(
            P(every, None),
            P("island", FSDP, None),
            P("island", None),
            P(None, FSDP),
            P(None, FSDP),
        ),
        check_vma=False,
    )
```

time: 157 us -> 104 us (0.66)
  the two profiles are of different devices: /device:TPU:2 before, /device:TPU:1 now
where the time goes in v2:
time: 104 us; the launch traced here: 103 us
  starting transfers between devices  70.2 us (68%)
  waiting for transfers between devices  12.2 us (12%)
  local copies, waits for them, and re-layouts  8.9 us (9%)
  Pallas kernels  7.7 us (7%)
  other arithmetic  3.54 us (3%)
    ppermute x10, starting transfers between devices, swap(): return lax.ppermute(value, axis, [(i, i ^ flip) for i in range(size)])  34.4 us
    all_to_all x2, starting transfers between devices, to_all(): lax.all_to_all(jnp.broadcast_to(value[None], (size,) + value.shape), axis...  24.4 us
    all_to_all x1, starting transfers between devices, shards(): chunks = lax.all_to_all(combined, 'zh', 0, 0)  11.4 us
    ppermute x10, waiting for transfers between devices, swap(): return lax.ppermute(value, axis, [(i, i ^ flip) for i in range(size)])  9.48 us
    unnamed x13, local copies, waits for them, and re-layouts  5.96 us
    pallas_call x1, Pallas kernels, project_forward(): pl.pallas_call(values_kernel, out_shape=jax.ShapeDtypeStruct((tokens, B),...  3.25 us
    all_to_all x1, waiting for transfers between devices, shards(): chunks = lax.all_to_all(combined, 'zh', 0, 0)  2.68 us
    broadcast_in_dim x2, local copies, waits for them, and re-layouts, to_all(): jnp.broadcast_to(value[None], (size,) + value.shape)  2.31 us
  transfers between devices with their start and end apart: 13, of which 4 were waited for; matrix products, arithmetic and copies ran while one was open for 4% of the time, Pallas kernels for 7%

profile of v2, /device:TPU:1, one launch (start us, length us, event | category | flops | bytes accessed | tf_op | source)
XLA Modules:
  0.0 103.4 jit_solution(7013102425691732689)
XLA Ops:
  0.6 0.0 copy-start.4
  0.7 1.7 %broadcast_in_dim.17 = bf16[16,128,128]{2,1,0:T(8,128)(2,1)} broadcast(bf16[128,128]{1,0:T(8,128)(2,1)} %bitcast.18), dimensions={1,2} | broadcast | bytes 557056 | tf_op jit(solution)/shard_map/weight_over_z/broadcast_in_dim | solution.py:27
  2.4 15.7 %all-to-all-start = ((bf16[16,128,128]{2,1,0:T(8,128)(2,1)}), bf16[16,128,128]{2,1,0:T(8,128)(2,1)S(1)}, u32[]{:S(2)}, u32[]{:S(2)}) async-start(bf16[16,128,128]{2,1,0:T(8,128)(2,1)} %broadcast_in_dim.17), calls=%async_computation | async-start | bytes 1048576 | tf_op jit(solution)/shard_map/weight_over_z/all_to_all | solution.py:27
  18.1 0.1 pad_add_fusion.place
  18.2 2.2 %copy-done = bf16[256,8192]{1,0:T(8,128)(2,1)S(1)} copy-done((bf16[256,8192]{1,0:T(8,128)(2,1)S(1)}, bf16[256,8192]{1,0:T(8,128)(2,1)}, u32[]{:S(2)}) %copy-start) | copy-done | bytes 4194328
  20.4 0.8 copy-done.2
  21.2 2.2 %project.1 = (bf16[4,8,128,128]{3,2,1,0:T(8,128)(2,1)S(1)}, bf16[4,8,128,128]{3,2,1,0:T(8,128)(2,1)S(1)}, f32[256,1]{1,0:T(8,128)S(1)}) custom-call(s32[2]{0:T(128)S(1)} %pad_add_fusion.place, bf16[256,8192]{1,0:T(8,128)(2,1)S(1)} %copy-done, bf16[256,128]{1,0:T(8,128)(2,1)S(1)} %copy-done.2), custom_call_target="tpu_custom_call" | custom-call | flops 536870912 | bytes 6291456 | tf_op jit(solution)/shard_map/projection_grad/project/pallas_call | solution.py:60
  23.4 2.9 %collective-permute-start.3 = (bf16[4,8,128,128]{3,2,1,0:T(8,128)(2,1)S(1)}, bf16[4,8,128,128]{3,2,1,0:T(8,128)(2,1)S(1)}, u32[]{:S(2)}, u32[]{:S(2)}) collective-permute-start(bf16[4,8,128,128]{3,2,1,0:T(8,128)(2,1)S(1)} %get-tuple-element.19), channel_id=1, source_target_pairs={{0,1},{1,0},{2,3},{3,2},{4,5},{5,4},{6,7},{7,6},{8,9},{9,8},{10,11... | collective-permute-start | bytes 3145736 | tf_op jit(solution)/shard_map/projection_grad/ppermute | solution.py:23
  26.3 2.3 %collective-permute-done.3.core_part = bf16[4,8,128,128]{3,2,1,0:T(8,128)(2,1)S(1)} collective-permute-done((bf16[4,8,128,128]{3,2,1,0:T(8,128)(2,1)S(1)}, bf16[4,8,128,128]{3,2,1,0:T(8,128)(2,1)S(1)}, u32[]{:S(2)}, u32[]{:S(2)}) %collective-permute-start.3) | collective-permute-done | bytes 1048608 | tf_op jit(solution)/shard_map/projection_grad/ppermute | solution.py:23
  28.6 0.8 merge.1
  29.4 4.6 %collective-permute-start.4 = (bf16[8,128,128]{2,1,0:T(8,128)(2,1)S(1)}, bf16[8,128,128]{2,1,0:T(8,128)(2,1)S(1)}, u32[]{:S(2)}, u32[]{:S(2)}) collective-permute-start(bf16[8,128,128]{2,1,0:T(8,128)(2,1)S(1)} %get-tuple-element.22), channel_id=1, source_target_pairs={{0,2},{2,0},{4,6},{6,4},{1,3},{3,1},{5,7},{7,5},{8,10},{10,8},{12,... | collective-permute-start | bytes 786440 | tf_op jit(solution)/shard_map/projection_grad/ppermute | solution.py:23
  34.0 3.5 %collective-permute-start.5 = (bf16[8,128,128]{2,1,0:T(8,128)(2,1)S(1)}, bf16[8,128,128]{2,1,0:T(8,128)(2,1)S(1)}, u32[]{:S(2)}, u32[]{:S(2)}) collective-permute-start(bf16[8,128,128]{2,1,0:T(8,128)(2,1)S(1)} %get-tuple-element.23), channel_id=1, source_target_pairs={{0,4},{2,6},{4,0},{6,2},{1,5},{3,7},{5,1},{7,3},{8,12},{10,14},{12... | collective-permute-start | bytes 786440 | tf_op jit(solution)/shard_map/projection_grad/ppermute | solution.py:23
  37.6 1.9 %collective-permute-start.6 = (bf16[8,128,128]{2,1,0:T(8,128)(2,1)S(1)}, bf16[8,128,128]{2,1,0:T(8,128)(2,1)S(1)}, u32[]{:S(2)}, u32[]{:S(2)}) collective-permute-start(bf16[8,128,128]{2,1,0:T(8,128)(2,1)S(1)} %get-tuple-element.24), channel_id=1, source_target_pairs={{0,6},{2,4},{4,2},{6,0},{1,7},{3,5},{5,3},{7,1},{8,14},{10,12},{12... | collective-permute-start | bytes 786440 | tf_op jit(solution)/shard_map/projection_grad/ppermute | solution.py:23
  39.5 3.2 %collective-permute-start.7 = (f32[64,448]{1,0:T(8,128)S(1)}, f32[64,448]{1,0:T(8,128)S(1)}, u32[]{:S(2)}, u32[]{:S(2)}) collective-permute-start(f32[64,448]{1,0:T(8,128)S(1)} %fusion.1), channel_id=1, source_target_pairs={{0,64},{64,0},{128,192},{192,128},{256,320},{320,256},{384,448},{4... | collective-permute-start | bytes 344072 | tf_op jit(solution)/shard_map/average_over_islands/ppermute | solution.py:23
  42.7 2.8 %collective-permute-done.7 = f32[64,448]{1,0:T(8,128)S(1)} collective-permute-done((f32[64,448]{1,0:T(8,128)S(1)}, f32[64,448]{1,0:T(8,128)S(1)}, u32[]{:S(2)}, u32[]{:S(2)}) %collective-permute-start.7) | collective-permute-done | bytes 114720 | tf_op jit(solution)/shard_map/average_over_islands/ppermute | solution.py:23
  45.6 4.6 %collective-permute-start.8 = (f32[64,448]{1,0:T(8,128)S(1)}, f32[64,448]{1,0:T(8,128)}, u32[]{:S(2)}, u32[]{:S(2)}) collective-permute-start(f32[64,448]{1,0:T(8,128)S(1)} %add.32), channel_id=1, source_target_pairs={{0,192},{64,128},{128,64},{192,0},{256,448},{320,384},{384,320},{4... | collective-permute-start | bytes 344072 | tf_op jit(solution)/shard_map/average_over_islands/ppermute | solution.py:23
  50.2 4.6 %collective-permute-start = (bf16[16,128,128]{2,1,0:T(8,128)(2,1)S(1)}, bf16[16,128,128]{2,1,0:T(8,128)(2,1)S(1)}, u32[]{:S(2)}, u32[]{:S(2)}) collective-permute-start(bf16[16,128,128]{2,1,0:T(8,128)(2,1)S(1)} %all-to-all-done.w00.weight), channel_id=1, source_target_pairs={{0,2},{2,0},{1,3},{3,1},{4,6},{6,4},{5,7},{7,5},{8,10},{10,8},{9,1... | collective-permute-start | bytes 1572872 | tf_op jit(solution)/shard_map/values/ppermute | solution.py:23
  54.8 1.6 %add.33 = f32[64,448]{1,0:T(8,128)} add(f32[64,448]{1,0:T(8,128)S(1)} %add.32, f32[64,448]{1,0:T(8,128)} %collective-permute-done.8) | non-fusion elementwise | flops 28672 | bytes 344064 | tf_op jit(solution)/shard_map/average_over_islands/add | solution.py:173
  56.4 1.5 %combine.1 = bf16[8,144,128]{2,1,0:T(8,128)(2,1)} custom-call(s32[2]{0:T(128)S(1)} %pad_add_fusion.place, f32[8,128,128]{2,1,0:T(8,128)S(1)} %get-tuple-element.21.own, bf16[8,128,128]{2,1,0:T(8,128)(2,1)S(1)} %collective-permute-done.4.one, bf16[8,128,128]{2,1,0:T(8,128)(2,1)S(1)} %collective-permute-done.5.two, ...), custom_call_target="tpu_custom_call" | custom-call | flops 786432 | bytes 1835008 | tf_op jit(solution)/shard_map/projection_grad/combine/pallas_call | solution.py:123
  57.9 11.4 %all-to-all-start.1 = ((bf16[8,144,128]{2,1,0:T(8,128)(2,1)}), bf16[8,144,128]{2,1,0:T(8,128)(2,1)S(1)}, u32[]{:S(2)}, u32[]{:S(2)}) async-start(bf16[8,144,128]{2,1,0:T(8,128)(2,1)} %combine.1), calls=%async_computation.1 | async-start | bytes 589824 | tf_op jit(solution)/shard_map/projection_grad/all_to_all | solution.py:199
  69.4 4.8 %collective-permute-start.1 = (bf16[16,128,128]{2,1,0:T(8,128)(2,1)S(1)}, bf16[16,128,128]{2,1,0:T(8,128)(2,1)S(1)}, u32[]{:S(2)}, u32[]{:S(2)}) collective-permute-start(bf16[16,128,128]{2,1,0:T(8,128)(2,1)S(1)} %all-to-all-done.w00.weight), channel_id=1, source_target_pairs={{0,1},{1,0},{2,3},{3,2},{4,5},{5,4},{6,7},{7,6},{8,9},{9,8},{10,11... | collective-permute-start | bytes 1572872 | tf_op jit(solution)/shard_map/values/ppermute | solution.py:23
  74.2 1.9 %collective-permute-start.2 = (bf16[16,128,128]{2,1,0:T(8,128)(2,1)S(1)}, bf16[16,128,128]{2,1,0:T(8,128)(2,1)S(1)}, u32[]{:S(2)}, u32[]{:S(2)}) collective-permute-start(bf16[16,128,128]{2,1,0:T(8,128)(2,1)S(1)} %collective-permute-done.w01), channel_id=1, source_target_pairs={{0,1},{1,0},{2,3},{3,2},{4,5},{5,4},{6,7},{7,6},{8,9},{9,8},{10,11... | collective-permute-start | bytes 1572872 | tf_op jit(solution)/shard_map/values/ppermute | solution.py:23
  76.1 2.2 %collective-permute-start.9 = (f32[64,448]{1,0:T(8,128)}, f32[64,448]{1,0:T(8,128)S(1)}, u32[]{:S(2)}, u32[]{:S(2)}) collective-permute-start(f32[64,448]{1,0:T(8,128)} %add.33), channel_id=1, source_target_pairs={{0,256},{64,320},{128,384},{192,448},{256,0},{320,64},{384,128},{4... | collective-permute-start | bytes 344072 | tf_op jit(solution)/shard_map/outer_update/ppermute | solution.py:23
  78.4 4.4 %collective-permute-done.9 = f32[64,448]{1,0:T(8,128)S(1)} collective-permute-done((f32[64,448]{1,0:T(8,128)}, f32[64,448]{1,0:T(8,128)S(1)}, u32[]{:S(2)}, u32[]{:S(2)}) %collective-permute-start.9) | collective-permute-done | bytes 114720 | tf_op jit(solution)/shard_map/outer_update/ppermute | solution.py:23
  82.8 1.8 %multiply_subtract_fusion = (f32[64,448]{1,0:T(8,128)}, f32[64,448]{1,0:T(8,128)}) fusion(f32[64,448]{1,0:T(8,128)} %param.11, f32[64,448]{1,0:T(8,128)} %add.33, f32[64,448]{1,0:T(8,128)S(1)} %collective-permute-done.9, f32[64,448]{1,0:T(8,128)} %param.13), kind=kLoop, calls=%fused_computation.3 | loop fusion | flops 229376 | bytes 688128 | tf_op jit(solution)/shard_map/outer_update/sub | solution.py:221
  84.6 2.7 %all-to-all-done.1 = bf16[8,144,128]{2,1,0:T(8,128)(2,1)S(1)} async-done(((bf16[8,144,128]{2,1,0:T(8,128)(2,1)}), bf16[8,144,128]{2,1,0:T(8,128)(2,1)S(1)}, u32[]{:S(2)}, u32[]{:S(2)}) %all-to-all-start.1) | async-done | bytes 294944 | tf_op jit(solution)/shard_map/projection_grad/all_to_all | solution.py:199
  87.3 0.6 broadcast_in_dim.19
  87.9 8.6 %all-to-all-start.2 = ((f32[8,8,128]{2,1,0:T(8,128)}), f32[8,8,128]{2,1,0:T(8,128)S(1)}, u32[]{:S(2)}, u32[]{:S(2)}) async-start(f32[8,8,128]{2,1,0:T(8,128)} %broadcast_in_dim.19), calls=%async_computation.2 | async-start | bytes 65536 | tf_op jit(solution)/shard_map/gain_grad/all_to_all | solution.py:27
  96.6 0.7 copy.14
  97.3 2.2 %copy-done.1 = bf16[256,8192]{1,0:T(8,128)(2,1)S(1)} copy-done((bf16[256,8192]{1,0:T(8,128)(2,1)S(1)}, bf16[256,8192]{1,0:T(8,128)(2,1)}, u32[]{:S(2)}) %copy-start.1) | copy-done | bytes 4194328
  99.5 3.2 %project_forward.1 = bf16[256,128]{1,0:T(8,128)(2,1)} custom-call(s32[2]{0:T(128)S(1)} %pad_add_fusion.place, bf16[256,8192]{1,0:T(8,128)(2,1)S(1)} %copy-done.1, f32[256,1]{1,0:T(8,128)S(1)} %get-tuple-element.17.inverse, f32[64,128]{1,0:T(8,128)S(1)} %bitcast.17, bf16[16,128,128]{2,1,0:T(8,128)(2,1)S(1)} %all-to-all-done.w00.weight, ...), custom_call_target="tpu_custom_call" | custom-call | flops 536870912 | bytes 6291456 | tf_op jit(solution)/shard_map/values/project_forward/pallas_call | solution.py:158
  102.7 0.6 copy.13
  (24 shorter events, 0.1 us)
Async XLA Ops:
  0.6 38.9 %copy-start.5 = (bf16[1,64,448]{2,1,0:T(8,128)(2,1)S(1)}, bf16[1,64,448]{2,1,0:T(8,128)(2,1)}, u32[]{:S(2)}) copy-start(bf16[1,64,448]{2,1,0:T(8,128)(2,1)} %param.12) | copy-start | bytes 172036
  0.6 38.9 %copy-start.4 = (f32[64,448]{1,0:T(8,128)S(1)}, f32[64,448]{1,0:T(8,128)}, u32[]{:S(2)}) copy-start(f32[64,448]{1,0:T(8,128)} %param.11) | copy-start | bytes 344068
  2.4 47.9 %all-to-all-start = ((bf16[16,128,128]{2,1,0:T(8,128)(2,1)}), bf16[16,128,128]{2,1,0:T(8,128)(2,1)S(1)}, u32[]{:S(2)}, u32[]{:S(2)}) async-start(bf16[16,128,128]{2,1,0:T(8,128)(2,1)} %broadcast_in_dim.17), calls=%async_computation | async-start | bytes 1048576 | tf_op jit(solution)/shard_map/weight_over_z/all_to_all | solution.py:27
  18.2 2.2 %copy-start = (bf16[256,8192]{1,0:T(8,128)(2,1)S(1)}, bf16[256,8192]{1,0:T(8,128)(2,1)}, u32[]{:S(2)}) copy-start(bf16[256,8192]{1,0:T(8,128)(2,1)} %x.3) | copy-start | bytes 12582916
  20.4 0.8 copy-start.2
  21.2 57.1 %copy-start.3 = (f32[1,8192]{1,0:T(1,128)S(1)}, f32[1,8192]{1,0:T(1,128)}, u32[]{:S(2)}) copy-start(f32[1,8192]{1,0:T(1,128)} %param.9) | copy-start | bytes 98308
  23.4 5.1 %collective-permute-start.3 = (bf16[4,8,128,128]{3,2,1,0:T(8,128)(2,1)S(1)}, bf16[4,8,128,128]{3,2,1,0:T(8,128)(2,1)S(1)}, u32[]{:S(2)}, u32[]{:S(2)}) collective-permute-start(bf16[4,8,128,128]{3,2,1,0:T(8,128)(2,1)S(1)} %get-tuple-element.19), channel_id=1, source_target_pairs={{0,1},{1,0},{2,3},{3,2},{4,5},{5,4},{6,7},{7,6},{8,9},{9,8},{10,11... | collective-permute-start | bytes 3145736 | tf_op jit(solution)/shard_map/projection_grad/ppermute | solution.py:23
  29.4 27.1 %collective-permute-start.4 = (bf16[8,128,128]{2,1,0:T(8,128)(2,1)S(1)}, bf16[8,128,128]{2,1,0:T(8,128)(2,1)S(1)}, u32[]{:S(2)}, u32[]{:S(2)}) collective-permute-start(bf16[8,128,128]{2,1,0:T(8,128)(2,1)S(1)} %get-tuple-element.22), channel_id=1, source_target_pairs={{0,2},{2,0},{4,6},{6,4},{1,3},{3,1},{5,7},{7,5},{8,10},{10,8},{12,... | collective-permute-start | bytes 786440 | tf_op jit(solution)/shard_map/projection_grad/ppermute | solution.py:23
  34.0 22.4 %collective-permute-start.5 = (bf16[8,128,128]{2,1,0:T(8,128)(2,1)S(1)}, bf16[8,128,128]{2,1,0:T(8,128)(2,1)S(1)}, u32[]{:S(2)}, u32[]{:S(2)}) collective-permute-start(bf16[8,128,128]{2,1,0:T(8,128)(2,1)S(1)} %get-tuple-element.23), channel_id=1, source_target_pairs={{0,4},{2,6},{4,0},{6,2},{1,5},{3,7},{5,1},{7,3},{8,12},{10,14},{12... | collective-permute-start | bytes 786440 | tf_op jit(solution)/shard_map/projection_grad/ppermute | solution.py:23
  37.6 18.9 %collective-permute-start.6 = (bf16[8,128,128]{2,1,0:T(8,128)(2,1)S(1)}, bf16[8,128,128]{2,1,0:T(8,128)(2,1)S(1)}, u32[]{:S(2)}, u32[]{:S(2)}) collective-permute-start(bf16[8,128,128]{2,1,0:T(8,128)(2,1)S(1)} %get-tuple-element.24), channel_id=1, source_target_pairs={{0,6},{2,4},{4,2},{6,0},{1,7},{3,5},{5,3},{7,1},{8,14},{10,12},{12... | collective-permute-start | bytes 786440 | tf_op jit(solution)/shard_map/projection_grad/ppermute | solution.py:23
  39.5 6.0 %collective-permute-start.7 = (f32[64,448]{1,0:T(8,128)S(1)}, f32[64,448]{1,0:T(8,128)S(1)}, u32[]{:S(2)}, u32[]{:S(2)}) collective-permute-start(f32[64,448]{1,0:T(8,128)S(1)} %fusion.1), channel_id=1, source_target_pairs={{0,64},{64,0},{128,192},{192,128},{256,320},{320,256},{384,448},{4... | collective-permute-start | bytes 344072 | tf_op jit(solution)/shard_map/average_over_islands/ppermute | solution.py:23
  45.6 9.3 %collective-permute-start.8 = (f32[64,448]{1,0:T(8,128)S(1)}, f32[64,448]{1,0:T(8,128)}, u32[]{:S(2)}, u32[]{:S(2)}) collective-permute-start(f32[64,448]{1,0:T(8,128)S(1)} %add.32), channel_id=1, source_target_pairs={{0,192},{64,128},{128,64},{192,0},{256,448},{320,384},{384,320},{4... | collective-permute-start | bytes 344072 | tf_op jit(solution)/shard_map/average_over_islands/ppermute | solution.py:23
  50.2 24.0 %collective-permute-start = (bf16[16,128,128]{2,1,0:T(8,128)(2,1)S(1)}, bf16[16,128,128]{2,1,0:T(8,128)(2,1)S(1)}, u32[]{:S(2)}, u32[]{:S(2)}) collective-permute-start(bf16[16,128,128]{2,1,0:T(8,128)(2,1)S(1)} %all-to-all-done.w00.weight), channel_id=1, source_target_pairs={{0,2},{2,0},{1,3},{3,1},{4,6},{6,4},{5,7},{7,5},{8,10},{10,8},{9,1... | collective-permute-start | bytes 1572872 | tf_op jit(solution)/shard_map/values/ppermute | solution.py:23
  57.9 29.3 %all-to-all-start.1 = ((bf16[8,144,128]{2,1,0:T(8,128)(2,1)}), bf16[8,144,128]{2,1,0:T(8,128)(2,1)S(1)}, u32[]{:S(2)}, u32[]{:S(2)}) async-start(bf16[8,144,128]{2,1,0:T(8,128)(2,1)} %combine.1), calls=%async_computation.1 | async-start | bytes 589824 | tf_op jit(solution)/shard_map/projection_grad/all_to_all | solution.py:199
  69.4 15.2 %collective-permute-start.1 = (bf16[16,128,128]{2,1,0:T(8,128)(2,1)S(1)}, bf16[16,128,128]{2,1,0:T(8,128)(2,1)S(1)}, u32[]{:S(2)}, u32[]{:S(2)}) collective-permute-start(bf16[16,128,128]{2,1,0:T(8,128)(2,1)S(1)} %all-to-all-done.w00.weight), channel_id=1, source_target_pairs={{0,1},{1,0},{2,3},{3,2},{4,5},{5,4},{6,7},{7,6},{8,9},{9,8},{10,11... | collective-permute-start | bytes 1572872 | tf_op jit(solution)/shard_map/values/ppermute | solution.py:23
  74.2 13.1 %collective-permute-start.2 = (bf16[16,128,128]{2,1,0:T(8,128)(2,1)S(1)}, bf16[16,128,128]{2,1,0:T(8,128)(2,1)S(1)}, u32[]{:S(2)}, u32[]{:S(2)}) collective-permute-start(bf16[16,128,128]{2,1,0:T(8,128)(2,1)S(1)} %collective-permute-done.w01), channel_id=1, source_target_pairs={{0,1},{1,0},{2,3},{3,2},{4,5},{5,4},{6,7},{7,6},{8,9},{9,8},{10,11... | collective-permute-start | bytes 1572872 | tf_op jit(solution)/shard_map/values/ppermute | solution.py:23
  76.1 6.7 %collective-permute-start.9 = (f32[64,448]{1,0:T(8,128)}, f32[64,448]{1,0:T(8,128)S(1)}, u32[]{:S(2)}, u32[]{:S(2)}) collective-permute-start(f32[64,448]{1,0:T(8,128)} %add.33), channel_id=1, source_target_pairs={{0,256},{64,320},{128,384},{192,448},{256,0},{320,64},{384,128},{4... | collective-permute-start | bytes 344072 | tf_op jit(solution)/shard_map/outer_update/ppermute | solution.py:23
  87.9 14.8 %all-to-all-start.2 = ((f32[8,8,128]{2,1,0:T(8,128)}), f32[8,8,128]{2,1,0:T(8,128)S(1)}, u32[]{:S(2)}, u32[]{:S(2)}) async-start(f32[8,8,128]{2,1,0:T(8,128)} %broadcast_in_dim.19), calls=%async_computation.2 | async-start | bytes 65536 | tf_op jit(solution)/shard_map/gain_grad/all_to_all | solution.py:27
  97.3 2.2 %copy-start.1 = (bf16[256,8192]{1,0:T(8,128)(2,1)S(1)}, bf16[256,8192]{1,0:T(8,128)(2,1)}, u32[]{:S(2)}) copy-start(bf16[256,8192]{1,0:T(8,128)(2,1)} %x.3) | copy-start | bytes 12582916

commit v3 on v2

--- a/solution.py
+++ b/solution.py
@@ -15,7 +15,6 @@
 f32, bf16 = jnp.float32, jnp.bfloat16
 SMEM = pl.BlockSpec(memory_space=pltpu.SMEM)
 VMEM = pl.BlockSpec(memory_space=pltpu.VMEM)
-LIMIT = 60 * 2**20
 SMALL = 20 * 2**20
 
 
@@ -29,6 +28,22 @@
 
 def whole(*shape):
     return pl.BlockSpec(shape, lambda *_: (0,) * len(shape))
+
+
+def spread_kernel(value, out):
+    for i in range(out.shape[0]):
+        out[i] = value[0]
+
+
+def spread(value, size):
+    return pl.pallas_call(
+        spread_kernel,
+        out_shape=jax.ShapeDtypeStruct((size,) + value.shape[1:], value.dtype),
+        in_specs=[VMEM],
+        out_specs=VMEM,
+        compiler_params=pltpu.CompilerParams(vmem_limit_bytes=SMALL),
+        name="spread",
+    )(value)
 
 
 def project_kernel(rows, place, x, cot, keep, send, inverse, scaled):
@@ -168,19 +183,13 @@
     )(place, activations, inverse, gain.reshape(-1, B), *pieces)
 
 
-def sum_over_islands(delta, islands, flips):
-    for flip in [f for f in flips if f < islands]:
-        delta = delta + swap(delta, "island", flip, islands)
-    return delta
-
-
 def shards(activations, cotangent, norm_gain, weight, global_slab, local_slab, momentum):
     quad, core = lax.axis_index(QUAD), lax.axis_index("core")
     depth, islands = lax.axis_size("zh"), lax.axis_size("island")
     place = jnp.stack([core, quad]).astype(jnp.int32)
 
     with jax.named_scope("weight_over_z"):
-        weight_z = to_all(weight[0], ("zh", "zl"), depth * ZL)
+        weight_z = lax.all_to_all(spread(weight, depth * ZL), ("zh", "zl"), 0, 0)
 
     with jax.named_scope("projection_grad"):
         keep, send, inverse = project(place, activations, cotangent)
@@ -188,23 +197,29 @@
         *sent, own = merge(place, keep, core_part)
         parts = [swap(part, QUAD, i, 4) for i, part in zip((1, 2, 3), sent)]
 
-    with jax.named_scope("average_over_islands"):
-        local, own = lax.optimization_barrier((local_slab, own))
-        delta = (global_slab - local[0].astype(f32)).astype(bf16)
-        average = sum_over_islands(delta.astype(f32), islands, (1, 3))
+    with jax.named_scope("deltas_over_islands"):
+        local = lax.optimization_barrier((local_slab, own))[0]
+        delta = (global_slab - local[0].astype(f32)).astype(bf16).astype(f32)
+        delta = delta + swap(delta, "island", 1, islands)
+        delta_y = swap(delta, "island", 3, islands)
 
     with jax.named_scope("projection_grad"):
         combined = combine(place, own, parts, weight_z)
-        combined, average = lax.optimization_barrier((combined, average))
+        combined, delta_y = lax.optimization_barrier((combined, delta_y))
         chunks = lax.all_to_all(combined, "zh", 0, 0)
 
     with jax.named_scope("values"):
-        w01 = swap(weight_z, "xh")
+        later = lax.optimization_barrier((weight_z, delta))[0]
+        w01 = swap(later, "xh")
         pieces = (weight_z, w01, swap(weight_z, "core"), swap(w01, "core"))
         values = project_forward(place, activations, inverse, norm_gain, pieces)
 
+    with jax.named_scope("deltas_over_islands"):
+        delta = delta + delta_y
+        delta_x = swap(delta, "island", 4, islands)
+
     with jax.named_scope("gain_grad"):
-        chunks, *rest = lax.optimization_barrier((chunks, pieces[2], pieces[3]))
+        chunks, values = lax.optimization_barrier((chunks, values))
         gain_grad = jnp.sum(chunks[:, B:].astype(f32), axis=0)
         gain_grad = gain_grad[:depth] + gain_grad[depth:]
         gain_grad = to_all(gain_grad, QUAD + ("core",), ZL * XH * CORE)
@@ -216,7 +231,8 @@
         weight_grad = (jnp.sum(chunks[:, :B].astype(f32), axis=0) * gain_own).T
 
     with jax.named_scope("outer_update"):
-        average = sum_over_islands(average, islands, (4,)) / islands
+        delta_x = lax.optimization_barrier((delta_x, chunks))[0]
+        average = (delta + delta_x) / islands
         new_momentum = 0.9 * momentum + average
         new_global = global_slab - 0.7 * (average + 0.9 * new_momentum)
 

time: 104 us -> 103 us (level)
  other arithmetic: 3.54 us -> 1.84 us
    all_to_all x0 -> x1, starting transfers between devices: none -> 15.7 us  [shards(): weight_z = lax.all_to_all(spread(weight, depth * ZL), ('zh', 'zl'), 0, 0)]
    all_to_all x2 -> x1, starting transfers between devices: 24.4 us -> 9.69 us  [to_all(): lax.all_to_all(jnp.broadcast_to(value[None], (size,) + value.shape), axis...]
    all_to_all x2 -> x1, waiting for transfers between devices: 0.01 us -> 4.07 us  [to_all(): lax.all_to_all(jnp.broadcast_to(value[None], (size,) + value.shape), axis...]
    ppermute x10, waiting for transfers between devices: 9.48 us -> 6.3 us  [swap(): return lax.ppermute(value, axis, [(i, i ^ flip) for i in range(size)])]
    broadcast_in_dim x2 -> x1, local copies, waits for them, and re-layouts: 2.31 us -> 0.62 us  [to_all(): jnp.broadcast_to(value[None], (size,) + value.shape)]
    unnamed x13 -> x19, local copies, waits for them, and re-layouts: 5.96 us -> 6.71 us
  transfers between devices with their start and end apart: 13 -> 13, of which waited for: 4 -> 5; matrix products, arithmetic and copies ran while one was open for 4% -> 3% of each run, Pallas kernels for 7% -> 8%
where the time goes in v3:
time: 103 us
  starting transfers between devices  70.2 us (68%)
  waiting for transfers between devices  13.1 us (13%)
  Pallas kernels  8.57 us (8%)
  local copies, waits for them, and re-layouts  7.96 us (8%)
  other arithmetic  1.84 us (2%)
    ppermute x10, starting transfers between devices, swap(): return lax.ppermute(value, axis, [(i, i ^ flip) for i in range(size)])  33.6 us
    all_to_all x1, starting transfers between devices, shards(): weight_z = lax.all_to_all(spread(weight, depth * ZL), ('zh', 'zl'), 0, 0)  15.7 us
    all_to_all x1, starting transfers between devices, shards(): chunks = lax.all_to_all(combined, 'zh', 0, 0)  11.2 us
    all_to_all x1, starting transfers between devices, to_all(): lax.all_to_all(jnp.broadcast_to(value[None], (size,) + value.shape), axis...  9.69 us
    unnamed x19, local copies, waits for them, and re-layouts  6.71 us
    ppermute x10, waiting for transfers between devices, swap(): return lax.ppermute(value, axis, [(i, i ^ flip) for i in range(size)])  6.3 us
    all_to_all x1, waiting for transfers between devices, to_all(): lax.all_to_all(jnp.broadcast_to(value[None], (size,) + value.shape), axis...  4.07 us
    pallas_call x1, Pallas kernels, project_forward(): pl.pallas_call(values_kernel, out_shape=jax.ShapeDtypeStruct((tokens, B),...  3.23 us
  transfers between devices with their start and end apart: 13, of which 5 were waited for; matrix products, arithmetic and copies ran while one was open for 3% of the time, Pallas kernels for 8%

profile of v3, /device:TPU:1, one launch (start us, length us, event | category | flops | bytes accessed | tf_op | source)
XLA Modules:
  0.0 102.5 jit_solution(9818066617458015142)
XLA Ops:
  0.6 0.7 copy-done.4
  1.4 0.9 spread.1
  2.3 15.7 %all-to-all-start = ((bf16[16,128,128]{2,1,0:T(8,128)(2,1)}), bf16[16,128,128]{2,1,0:T(8,128)(2,1)S(1)}, u32[]{:S(2)}, u32[]{:S(2)}) async-start(bf16[16,128,128]{2,1,0:T(8,128)(2,1)} %spread.1), calls=%async_computation | async-start | bytes 1048576 | tf_op jit(solution)/shard_map/weight_over_z/all_to_all | solution.py:192
  18.1 2.2 %copy-done = bf16[256,8192]{1,0:T(8,128)(2,1)S(1)} copy-done((bf16[256,8192]{1,0:T(8,128)(2,1)S(1)}, bf16[256,8192]{1,0:T(8,128)(2,1)}, u32[]{:S(2)}) %copy-start) | copy-done | bytes 4194328
  20.3 0.8 copy-done.2
  21.1 2.2 %project.1 = (bf16[4,8,128,128]{3,2,1,0:T(8,128)(2,1)S(1)}, bf16[4,8,128,128]{3,2,1,0:T(8,128)(2,1)S(1)}, f32[256,1]{1,0:T(8,128)S(1)}) custom-call(s32[2]{0:T(128)S(1)} %pad_add_fusion.place, bf16[256,8192]{1,0:T(8,128)(2,1)S(1)} %copy-done, bf16[256,128]{1,0:T(8,128)(2,1)S(1)} %copy-done.2), custom_call_target="tpu_custom_call" | custom-call | flops 536870912 | bytes 6291456 | tf_op jit(solution)/shard_map/projection_grad/project/pallas_call | solution.py:75
  23.3 2.9 %collective-permute-start = (bf16[4,8,128,128]{3,2,1,0:T(8,128)(2,1)S(1)}, bf16[4,8,128,128]{3,2,1,0:T(8,128)(2,1)S(1)}, u32[]{:S(2)}, u32[]{:S(2)}) collective-permute-start(bf16[4,8,128,128]{3,2,1,0:T(8,128)(2,1)S(1)} %get-tuple-element.20), channel_id=1, source_target_pairs={{0,1},{1,0},{2,3},{3,2},{4,5},{5,4},{6,7},{7,6},{8,9},{9,8},{10,11... | collective-permute-start | bytes 3145736 | tf_op jit(solution)/shard_map/projection_grad/ppermute | solution.py:22
  26.2 2.3 %collective-permute-done.core_part = bf16[4,8,128,128]{3,2,1,0:T(8,128)(2,1)S(1)} collective-permute-done((bf16[4,8,128,128]{3,2,1,0:T(8,128)(2,1)S(1)}, bf16[4,8,128,128]{3,2,1,0:T(8,128)(2,1)S(1)}, u32[]{:S(2)}, u32[]{:S(2)}) %collective-permute-start) | collective-permute-done | bytes 1048608 | tf_op jit(solution)/shard_map/projection_grad/ppermute | solution.py:22
  28.5 0.8 merge.1
  29.3 4.7 %collective-permute-start.1 = (bf16[8,128,128]{2,1,0:T(8,128)(2,1)S(1)}, bf16[8,128,128]{2,1,0:T(8,128)(2,1)S(1)}, u32[]{:S(2)}, u32[]{:S(2)}) collective-permute-start(bf16[8,128,128]{2,1,0:T(8,128)(2,1)S(1)} %get-tuple-element.22), channel_id=1, source_target_pairs={{0,2},{2,0},{4,6},{6,4},{1,3},{3,1},{5,7},{7,5},{8,10},{10,8},{12,... | collective-permute-start | bytes 786440 | tf_op jit(solution)/shard_map/projection_grad/ppermute | solution.py:22
  33.9 3.5 %collective-permute-start.2 = (bf16[8,128,128]{2,1,0:T(8,128)(2,1)S(1)}, bf16[8,128,128]{2,1,0:T(8,128)(2,1)S(1)}, u32[]{:S(2)}, u32[]{:S(2)}) collective-permute-start(bf16[8,128,128]{2,1,0:T(8,128)(2,1)S(1)} %get-tuple-element.23), channel_id=1, source_target_pairs={{0,4},{2,6},{4,0},{6,2},{1,5},{3,7},{5,1},{7,3},{8,12},{10,14},{12... | collective-permute-start | bytes 786440 | tf_op jit(solution)/shard_map/projection_grad/ppermute | solution.py:22
  37.5 1.9 %collective-permute-start.3 = (bf16[8,128,128]{2,1,0:T(8,128)(2,1)S(1)}, bf16[8,128,128]{2,1,0:T(8,128)(2,1)S(1)}, u32[]{:S(2)}, u32[]{:S(2)}) collective-permute-start(bf16[8,128,128]{2,1,0:T(8,128)(2,1)S(1)} %get-tuple-element.24), channel_id=1, source_target_pairs={{0,6},{2,4},{4,2},{6,0},{1,7},{3,5},{5,3},{7,1},{8,14},{10,12},{12... | collective-permute-start | bytes 786440 | tf_op jit(solution)/shard_map/projection_grad/ppermute | solution.py:22
  39.5 3.2 %collective-permute-start.4 = (f32[64,448]{1,0:T(8,128)S(1)}, f32[64,448]{1,0:T(8,128)S(1)}, u32[]{:S(2)}, u32[]{:S(2)}) collective-permute-start(f32[64,448]{1,0:T(8,128)S(1)} %fusion.1), channel_id=1, source_target_pairs={{0,64},{64,0},{128,192},{192,128},{256,320},{320,256},{384,448},{4... | collective-permute-start | bytes 344072 | tf_op jit(solution)/shard_map/deltas_over_islands/ppermute | solution.py:22
  42.7 2.8 %collective-permute-done.4 = f32[64,448]{1,0:T(8,128)S(1)} collective-permute-done((f32[64,448]{1,0:T(8,128)S(1)}, f32[64,448]{1,0:T(8,128)S(1)}, u32[]{:S(2)}, u32[]{:S(2)}) %collective-permute-start.4) | collective-permute-done | bytes 114720 | tf_op jit(solution)/shard_map/deltas_over_islands/ppermute | solution.py:22
  45.5 4.6 %collective-permute-start.5 = (f32[64,448]{1,0:T(8,128)S(1)}, f32[64,448]{1,0:T(8,128)}, u32[]{:S(2)}, u32[]{:S(2)}) collective-permute-start(f32[64,448]{1,0:T(8,128)S(1)} %add.32), channel_id=1, source_target_pairs={{0,192},{64,128},{128,64},{192,0},{256,448},{320,384},{384,320},{4... | collective-permute-start | bytes 344072 | tf_op jit(solution)/shard_map/deltas_over_islands/ppermute | solution.py:22
  50.1 4.6 %collective-permute-start.6 = (bf16[16,128,128]{2,1,0:T(8,128)(2,1)S(1)}, bf16[16,128,128]{2,1,0:T(8,128)(2,1)S(1)}, u32[]{:S(2)}, u32[]{:S(2)}) collective-permute-start(bf16[16,128,128]{2,1,0:T(8,128)(2,1)S(1)} %all-to-all-done.weight.w00), channel_id=1, source_target_pairs={{0,2},{2,0},{1,3},{3,1},{4,6},{6,4},{5,7},{7,5},{8,10},{10,8},{9,1... | collective-permute-start | bytes 1572872 | tf_op jit(solution)/shard_map/values/ppermute | solution.py:22
  54.8 1.2 %collective-permute-done.3.three = bf16[8,128,128]{2,1,0:T(8,128)(2,1)S(1)} collective-permute-done((bf16[8,128,128]{2,1,0:T(8,128)(2,1)S(1)}, bf16[8,128,128]{2,1,0:T(8,128)(2,1)S(1)}, u32[]{:S(2)}, u32[]{:S(2)}) %collective-permute-start.3) | collective-permute-done | bytes 262176 | tf_op jit(solution)/shard_map/projection_grad/ppermute | solution.py:22
  56.0 1.5 %combine.1 = bf16[8,144,128]{2,1,0:T(8,128)(2,1)} custom-call(s32[2]{0:T(128)S(1)} %pad_add_fusion.place, f32[8,128,128]{2,1,0:T(8,128)S(1)} %get-tuple-element.21.own, bf16[8,128,128]{2,1,0:T(8,128)(2,1)S(1)} %collective-permute-done.1.one, bf16[8,128,128]{2,1,0:T(8,128)(2,1)S(1)} %collective-permute-done.2.two, ...), custom_call_target="tpu_custom_call" | custom-call | flops 786432 | bytes 1835008 | tf_op jit(solution)/shard_map/projection_grad/combine/pallas_call | solution.py:138
  57.5 11.2 %all-to-all-start.1 = ((bf16[8,144,128]{2,1,0:T(8,128)(2,1)}), bf16[8,144,128]{2,1,0:T(8,128)(2,1)S(1)}, u32[]{:S(2)}, u32[]{:S(2)}) async-start(bf16[8,144,128]{2,1,0:T(8,128)(2,1)} %combine.1), calls=%async_computation.1 | async-start | bytes 589824 | tf_op jit(solution)/shard_map/projection_grad/all_to_all | solution.py:209
  68.7 4.0 %collective-permute-start.7 = (bf16[16,128,128]{2,1,0:T(8,128)(2,1)S(1)}, bf16[16,128,128]{2,1,0:T(8,128)(2,1)S(1)}, u32[]{:S(2)}, u32[]{:S(2)}) collective-permute-start(bf16[16,128,128]{2,1,0:T(8,128)(2,1)S(1)} %all-to-all-done.weight.w00), channel_id=1, source_target_pairs={{0,1},{1,0},{2,3},{3,2},{4,5},{5,4},{6,7},{7,6},{8,9},{9,8},{10,11... | collective-permute-start | bytes 1572872 | tf_op jit(solution)/shard_map/values/ppermute | solution.py:22
  72.7 1.9 %collective-permute-start.8 = (bf16[16,128,128]{2,1,0:T(8,128)(2,1)S(1)}, bf16[16,128,128]{2,1,0:T(8,128)(2,1)S(1)}, u32[]{:S(2)}, u32[]{:S(2)}) collective-permute-start(bf16[16,128,128]{2,1,0:T(8,128)(2,1)S(1)} %collective-permute-done.6.w01), channel_id=1, source_target_pairs={{0,1},{1,0},{2,3},{3,2},{4,5},{5,4},{6,7},{7,6},{8,9},{9,8},{10,11... | collective-permute-start | bytes 1572872 | tf_op jit(solution)/shard_map/values/ppermute | solution.py:22
  74.7 0.9 add.37
  75.6 2.2 %collective-permute-start.9 = (f32[64,448]{1,0:T(8,128)S(1)}, f32[64,448]{1,0:T(8,128)S(1)}, u32[]{:S(2)}, u32[]{:S(2)}) collective-permute-start(f32[64,448]{1,0:T(8,128)S(1)} %add.37), channel_id=1, source_target_pairs={{0,256},{64,320},{128,384},{192,448},{256,0},{320,64},{384,128},{4... | collective-permute-start | bytes 344072 | tf_op jit(solution)/shard_map/deltas_over_islands/ppermute | solution.py:22
  77.8 2.2 %copy-done.1 = bf16[256,8192]{1,0:T(8,128)(2,1)S(1)} copy-done((bf16[256,8192]{1,0:T(8,128)(2,1)S(1)}, bf16[256,8192]{1,0:T(8,128)(2,1)}, u32[]{:S(2)}) %copy-start.1) | copy-done | bytes 4194328
  80.0 3.2 %project_forward.1 = bf16[256,128]{1,0:T(8,128)(2,1)} custom-call(s32[2]{0:T(128)S(1)} %pad_add_fusion.place, bf16[256,8192]{1,0:T(8,128)(2,1)S(1)} %copy-done.1, f32[256,1]{1,0:T(8,128)S(1)} %get-tuple-element.27.inverse, f32[64,128]{1,0:T(8,128)S(1)} %bitcast.16, bf16[16,128,128]{2,1,0:T(8,128)(2,1)S(1)} %all-to-all-done.weight.w00, ...), custom_call_target="tpu_custom_call" | custom-call | flops 536870912 | bytes 6291456 | tf_op jit(solution)/shard_map/values/project_forward/pallas_call | solution.py:173
  83.2 2.7 %all-to-all-done.1 = bf16[8,144,128]{2,1,0:T(8,128)(2,1)S(1)} async-done(((bf16[8,144,128]{2,1,0:T(8,128)(2,1)}), bf16[8,144,128]{2,1,0:T(8,128)(2,1)S(1)}, u32[]{:S(2)}, u32[]{:S(2)}) %all-to-all-start.1) | async-done | bytes 294944 | tf_op jit(solution)/shard_map/projection_grad/all_to_all | solution.py:209
  86.0 0.6 broadcast_in_dim.10
  86.6 9.7 %all-to-all-start.2 = ((f32[8,8,128]{2,1,0:T(8,128)}), f32[8,8,128]{2,1,0:T(8,128)S(1)}, u32[]{:S(2)}, u32[]{:S(2)}) async-start(f32[8,8,128]{2,1,0:T(8,128)} %broadcast_in_dim.10), calls=%async_computation.2 | async-start | bytes 65536 | tf_op jit(solution)/shard_map/gain_grad/all_to_all | solution.py:26
  96.3 0.7 multiply_subtract_fusion
  97.1 0.7 copy.14
  97.8 4.1 %all-to-all-done.2 = f32[8,8,128]{2,1,0:T(8,128)S(1)} async-done(((f32[8,8,128]{2,1,0:T(8,128)}), f32[8,8,128]{2,1,0:T(8,128)S(1)}, u32[]{:S(2)}, u32[]{:S(2)}) %all-to-all-start.2) | async-done | bytes 32800 | tf_op jit(solution)/shard_map/gain_grad/all_to_all | solution.py:26
  101.9 0.6 copy.13
  (30 shorter events, 0.2 us)
Async XLA Ops:
  0.6 0.8 copy-start.4
  1.4 38.0 %copy-start.5 = (f32[64,448]{1,0:T(8,128)S(1)}, f32[64,448]{1,0:T(8,128)}, u32[]{:S(2)}) copy-start(f32[64,448]{1,0:T(8,128)} %param.11) | copy-start | bytes 344068
  1.4 38.0 %copy-start.8 = (bf16[1,64,448]{2,1,0:T(8,128)(2,1)S(1)}, bf16[1,64,448]{2,1,0:T(8,128)(2,1)}, u32[]{:S(2)}) copy-start(bf16[1,64,448]{2,1,0:T(8,128)(2,1)} %param.12) | copy-start | bytes 172036
  2.3 47.9 %all-to-all-start = ((bf16[16,128,128]{2,1,0:T(8,128)(2,1)}), bf16[16,128,128]{2,1,0:T(8,128)(2,1)S(1)}, u32[]{:S(2)}, u32[]{:S(2)}) async-start(bf16[16,128,128]{2,1,0:T(8,128)(2,1)} %spread.1), calls=%async_computation | async-start | bytes 1048576 | tf_op jit(solution)/shard_map/weight_over_z/all_to_all | solution.py:192
  18.1 2.2 %copy-start = (bf16[256,8192]{1,0:T(8,128)(2,1)S(1)}, bf16[256,8192]{1,0:T(8,128)(2,1)}, u32[]{:S(2)}) copy-start(bf16[256,8192]{1,0:T(8,128)(2,1)} %x.3) | copy-start | bytes 12582916
  20.3 0.8 copy-start.2
  21.1 53.5 %copy-start.3 = (f32[1,8192]{1,0:T(1,128)S(1)}, f32[1,8192]{1,0:T(1,128)}, u32[]{:S(2)}) copy-start(f32[1,8192]{1,0:T(1,128)} %param.9) | copy-start | bytes 98308
  23.3 5.1 %collective-permute-start = (bf16[4,8,128,128]{3,2,1,0:T(8,128)(2,1)S(1)}, bf16[4,8,128,128]{3,2,1,0:T(8,128)(2,1)S(1)}, u32[]{:S(2)}, u32[]{:S(2)}) collective-permute-start(bf16[4,8,128,128]{3,2,1,0:T(8,128)(2,1)S(1)} %get-tuple-element.20), channel_id=1, source_target_pairs={{0,1},{1,0},{2,3},{3,2},{4,5},{5,4},{6,7},{7,6},{8,9},{9,8},{10,11... | collective-permute-start | bytes 3145736 | tf_op jit(solution)/shard_map/projection_grad/ppermute | solution.py:22
  29.3 25.5 %collective-permute-start.1 = (bf16[8,128,128]{2,1,0:T(8,128)(2,1)S(1)}, bf16[8,128,128]{2,1,0:T(8,128)(2,1)S(1)}, u32[]{:S(2)}, u32[]{:S(2)}) collective-permute-start(bf16[8,128,128]{2,1,0:T(8,128)(2,1)S(1)} %get-tuple-element.22), channel_id=1, source_target_pairs={{0,2},{2,0},{4,6},{6,4},{1,3},{3,1},{5,7},{7,5},{8,10},{10,8},{12,... | collective-permute-start | bytes 786440 | tf_op jit(solution)/shard_map/projection_grad/ppermute | solution.py:22
  33.9 20.8 %collective-permute-start.2 = (bf16[8,128,128]{2,1,0:T(8,128)(2,1)S(1)}, bf16[8,128,128]{2,1,0:T(8,128)(2,1)S(1)}, u32[]{:S(2)}, u32[]{:S(2)}) collective-permute-start(bf16[8,128,128]{2,1,0:T(8,128)(2,1)S(1)} %get-tuple-element.23), channel_id=1, source_target_pairs={{0,4},{2,6},{4,0},{6,2},{1,5},{3,7},{5,1},{7,3},{8,12},{10,14},{12... | collective-permute-start | bytes 786440 | tf_op jit(solution)/shard_map/projection_grad/ppermute | solution.py:22
  37.5 18.5 %collective-permute-start.3 = (bf16[8,128,128]{2,1,0:T(8,128)(2,1)S(1)}, bf16[8,128,128]{2,1,0:T(8,128)(2,1)S(1)}, u32[]{:S(2)}, u32[]{:S(2)}) collective-permute-start(bf16[8,128,128]{2,1,0:T(8,128)(2,1)S(1)} %get-tuple-element.24), channel_id=1, source_target_pairs={{0,6},{2,4},{4,2},{6,0},{1,7},{3,5},{5,3},{7,1},{8,14},{10,12},{12... | collective-permute-start | bytes 786440 | tf_op jit(solution)/shard_map/projection_grad/ppermute | solution.py:22
  39.5 6.0 %collective-permute-start.4 = (f32[64,448]{1,0:T(8,128)S(1)}, f32[64,448]{1,0:T(8,128)S(1)}, u32[]{:S(2)}, u32[]{:S(2)}) collective-permute-start(f32[64,448]{1,0:T(8,128)S(1)} %fusion.1), channel_id=1, source_target_pairs={{0,64},{64,0},{128,192},{192,128},{256,320},{320,256},{384,448},{4... | collective-permute-start | bytes 344072 | tf_op jit(solution)/shard_map/deltas_over_islands/ppermute | solution.py:22
  45.5 12.0 %collective-permute-start.5 = (f32[64,448]{1,0:T(8,128)S(1)}, f32[64,448]{1,0:T(8,128)}, u32[]{:S(2)}, u32[]{:S(2)}) collective-permute-start(f32[64,448]{1,0:T(8,128)S(1)} %add.32), channel_id=1, source_target_pairs={{0,192},{64,128},{128,64},{192,0},{256,448},{320,384},{384,320},{4... | collective-permute-start | bytes 344072 | tf_op jit(solution)/shard_map/deltas_over_islands/ppermute | solution.py:22
  50.1 22.5 %collective-permute-start.6 = (bf16[16,128,128]{2,1,0:T(8,128)(2,1)S(1)}, bf16[16,128,128]{2,1,0:T(8,128)(2,1)S(1)}, u32[]{:S(2)}, u32[]{:S(2)}) collective-permute-start(bf16[16,128,128]{2,1,0:T(8,128)(2,1)S(1)} %all-to-all-done.weight.w00), channel_id=1, source_target_pairs={{0,2},{2,0},{1,3},{3,1},{4,6},{6,4},{5,7},{7,5},{8,10},{10,8},{9,1... | collective-permute-start | bytes 1572872 | tf_op jit(solution)/shard_map/values/ppermute | solution.py:22
  57.5 38.9 %copy-start.6 = (f32[64,448]{1,0:T(8,128)S(1)}, f32[64,448]{1,0:T(8,128)}, u32[]{:S(2)}) copy-start(f32[64,448]{1,0:T(8,128)} %param.11) | copy-start | bytes 344068
  57.5 38.9 %copy-start.7 = (f32[64,448]{1,0:T(8,128)S(1)}, f32[64,448]{1,0:T(8,128)}, u32[]{:S(2)}) copy-start(f32[64,448]{1,0:T(8,128)} %param.13) | copy-start | bytes 344068
  57.5 28.5 %all-to-all-start.1 = ((bf16[8,144,128]{2,1,0:T(8,128)(2,1)}), bf16[8,144,128]{2,1,0:T(8,128)(2,1)S(1)}, u32[]{:S(2)}, u32[]{:S(2)}) async-start(bf16[8,144,128]{2,1,0:T(8,128)(2,1)} %combine.1), calls=%async_computation.1 | async-start | bytes 589824 | tf_op jit(solution)/shard_map/projection_grad/all_to_all | solution.py:209
  68.7 9.2 %collective-permute-start.7 = (bf16[16,128,128]{2,1,0:T(8,128)(2,1)S(1)}, bf16[16,128,128]{2,1,0:T(8,128)(2,1)S(1)}, u32[]{:S(2)}, u32[]{:S(2)}) collective-permute-start(bf16[16,128,128]{2,1,0:T(8,128)(2,1)S(1)} %all-to-all-done.weight.w00), channel_id=1, source_target_pairs={{0,1},{1,0},{2,3},{3,2},{4,5},{5,4},{6,7},{7,6},{8,9},{9,8},{10,11... | collective-permute-start | bytes 1572872 | tf_op jit(solution)/shard_map/values/ppermute | solution.py:22
  72.7 5.1 %collective-permute-start.8 = (bf16[16,128,128]{2,1,0:T(8,128)(2,1)S(1)}, bf16[16,128,128]{2,1,0:T(8,128)(2,1)S(1)}, u32[]{:S(2)}, u32[]{:S(2)}) collective-permute-start(bf16[16,128,128]{2,1,0:T(8,128)(2,1)S(1)} %collective-permute-done.6.w01), channel_id=1, source_target_pairs={{0,1},{1,0},{2,3},{3,2},{4,5},{5,4},{6,7},{7,6},{8,9},{9,8},{10,11... | collective-permute-start | bytes 1572872 | tf_op jit(solution)/shard_map/values/ppermute | solution.py:22
  75.6 10.4 %collective-permute-start.9 = (f32[64,448]{1,0:T(8,128)S(1)}, f32[64,448]{1,0:T(8,128)S(1)}, u32[]{:S(2)}, u32[]{:S(2)}) collective-permute-start(f32[64,448]{1,0:T(8,128)S(1)} %add.37), channel_id=1, source_target_pairs={{0,256},{64,320},{128,384},{192,448},{256,0},{320,64},{384,128},{4... | collective-permute-start | bytes 344072 | tf_op jit(solution)/shard_map/deltas_over_islands/ppermute | solution.py:22
  77.8 2.2 %copy-start.1 = (bf16[256,8192]{1,0:T(8,128)(2,1)S(1)}, bf16[256,8192]{1,0:T(8,128)(2,1)}, u32[]{:S(2)}) copy-start(bf16[256,8192]{1,0:T(8,128)(2,1)} %x.3) | copy-start | bytes 12582916
  86.6 15.3 %all-to-all-start.2 = ((f32[8,8,128]{2,1,0:T(8,128)}), f32[8,8,128]{2,1,0:T(8,128)S(1)}, u32[]{:S(2)}, u32[]{:S(2)}) async-start(f32[8,8,128]{2,1,0:T(8,128)} %broadcast_in_dim.10), calls=%async_computation.2 | async-start | bytes 65536 | tf_op jit(solution)/shard_map/gain_grad/all_to_all | solution.py:26

commit v4 on v3

--- a/solution.py
+++ b/solution.py
@@ -13,7 +13,6 @@
 ZL = XH = CORE = 2
 B = 128
 f32, bf16 = jnp.float32, jnp.bfloat16
-SMEM = pl.BlockSpec(memory_space=pltpu.SMEM)
 VMEM = pl.BlockSpec(memory_space=pltpu.VMEM)
 SMALL = 20 * 2**20
 
@@ -46,7 +45,7 @@
     )(value)
 
 
-def project_kernel(rows, place, x, cot, keep, send, inverse, scaled):
+def project_kernel(rows, x, cot, keep, send, inverse, scaled):
     tokens, width = x.shape
     for i in range(0, tokens, rows):
         total = jnp.zeros((rows, B), f32)
@@ -58,7 +57,7 @@
         inverse[pl.ds(i, rows), :] = unit
         scaled[pl.ds(i, rows), :] = cot[pl.ds(i, rows), :].astype(f32) * unit
     left = scaled[...].T.astype(bf16)
-    core = place[0]
+    core = lax.axis_index("core")
     for k in range(width // (CORE * B)):
         both = jnp.dot(left, x[:, pl.ds(k * CORE * B, CORE * B)], preferred_element_type=f32)
         both = both.astype(bf16)
@@ -68,14 +67,14 @@
         send[at, z] = jnp.where(core == 0, second, first)
 
 
-def project(place, activations, cotangent):
+def project(activations, cotangent):
     tokens, width = activations.shape
     rows = 32
     half = jax.ShapeDtypeStruct((ZL * XH, width // (ZL * XH * CORE * B), B, B), bf16)
     return pl.pallas_call(
         functools.partial(project_kernel, rows),
         out_shape=(half, half, jax.ShapeDtypeStruct((tokens, 1), f32)),
-        in_specs=[SMEM, VMEM, VMEM],
+        in_specs=[VMEM, VMEM],
         out_specs=[VMEM] * 3,
         scratch_shapes=[
             pltpu.VMEM((tokens, B), f32),
@@ -85,7 +84,7 @@
             flops=2 * tokens * width * B, bytes_accessed=3 * tokens * width, transcendentals=0
         ),
         name="project",
-    )(place, activations, cotangent)
+    )(activations, cotangent)
 
 
 def relative(i, quad):
@@ -93,34 +92,34 @@
     return (1 - high if i // 2 else high) * 2 + (1 - low if i % 2 else low)
 
 
-def merge_kernel(place, keep, core_part, one, two, three, own):
-    for i, out in enumerate((own, one, two, three)):
-        at = relative(i, place[1])
+def merge_kernel(keep, core_part, both, xh, zl, own):
+    for i, out in ((0, own), (3, both), (1, xh), (2, zl)):
+        at = relative(i, lax.axis_index(QUAD))
         for z in range(keep.shape[1]):
             total = keep[at, z].astype(f32) + core_part[at, z].astype(f32)
             out[z] = total.astype(out.dtype)
 
 
-def merge(place, keep, core_part):
+def merge(keep, core_part):
     quad, z = keep.shape[:2]
     block = jax.ShapeDtypeStruct((z, B, B), bf16)
     return pl.pallas_call(
         merge_kernel,
         grid=(1,),
         out_shape=(block,) * 3 + (jax.ShapeDtypeStruct((z, B, B), f32),),
-        in_specs=[SMEM] + [whole(*keep.shape)] * 2,
+        in_specs=[whole(*keep.shape)] * 2,
         out_specs=[whole(z, B, B)] * 4,
         compiler_params=pltpu.CompilerParams(vmem_limit_bytes=SMALL),
         cost_estimate=pl.CostEstimate(
             flops=quad * z * B * B, bytes_accessed=7 * quad * z * B * B, transcendentals=0
         ),
         name="merge",
-    )(place, keep, core_part)
-
-
-def combine_kernel(place, own, one, two, three, weight, out, gain):
+    )(keep, core_part)
+
+
+def combine_kernel(own, one, two, three, weight, out, gain):
     depth = own.shape[0]
-    zl = place[1] // XH
+    zl = lax.axis_index(QUAD) // XH
     for z in range(depth):
         total = own[z] + one[z].astype(f32) + two[z].astype(f32) + three[z].astype(f32)
         out[z, pl.ds(0, B), :] = total.astype(bf16)
@@ -133,13 +132,13 @@
         out[z, pl.ds(B, 2 * depth), :] = terms
 
 
-def combine(place, own, parts, weight):
+def combine(own, parts, weight):
     z = own.shape[0]
     return pl.pallas_call(
         combine_kernel,
         grid=(1,),
         out_shape=jax.ShapeDtypeStruct((z, B + 2 * z, B), bf16),
-        in_specs=[SMEM] + [whole(z, B, B)] * 4 + [whole(ZL * z, B, B)],
+        in_specs=[whole(z, B, B)] * 4 + [whole(ZL * z, B, B)],
         out_specs=whole(z, B + 2 * z, B),
         scratch_shapes=[pltpu.VMEM((z, B), f32)],
         compiler_params=pltpu.CompilerParams(vmem_limit_bytes=SMALL),
@@ -147,12 +146,12 @@
             flops=6 * z * B * B, bytes_accessed=14 * z * B * B, transcendentals=0
         ),
         name="combine",
-    )(place, own, *parts, weight)
-
-
-def values_kernel(place, x, inverse, gain, w00, w01, w10, w11, out):
-    core = place[0]
-    same = place[1] % XH == 0
+    )(own, *parts, weight)
+
+
+def values_kernel(x, inverse, gain, w00, w01, w10, w11, out):
+    core = lax.axis_index("core")
+    same = lax.axis_index(QUAD) % XH == 0
     column = gain[...].T
     total = jnp.zeros(out.shape, f32)
     for k in range(x.shape[1] // (CORE * B)):
@@ -168,34 +167,33 @@
     out[...] = (total * inverse[...]).astype(bf16)
 
 
-def project_forward(place, activations, inverse, gain, pieces):
+def project_forward(activations, inverse, gain, pieces):
     tokens, width = activations.shape
     return pl.pallas_call(
         values_kernel,
         out_shape=jax.ShapeDtypeStruct((tokens, B), bf16),
-        in_specs=[SMEM] + [VMEM] * 7,
+        in_specs=[VMEM] * 7,
         out_specs=VMEM,
         compiler_params=pltpu.CompilerParams(vmem_limit_bytes=SMALL),
         cost_estimate=pl.CostEstimate(
             flops=2 * tokens * width * B, bytes_accessed=3 * tokens * width, transcendentals=0
         ),
         name="project_forward",
-    )(place, activations, inverse, gain.reshape(-1, B), *pieces)
+    )(activations, inverse, gain.reshape(-1, B), *pieces)
 
 
 def shards(activations, cotangent, norm_gain, weight, global_slab, local_slab, momentum):
     quad, core = lax.axis_index(QUAD), lax.axis_index("core")
     depth, islands = lax.axis_size("zh"), lax.axis_size("island")
-    place = jnp.stack([core, quad]).astype(jnp.int32)
 
     with jax.named_scope("weight_over_z"):
         weight_z = lax.all_to_all(spread(weight, depth * ZL), ("zh", "zl"), 0, 0)
 
     with jax.named_scope("projection_grad"):
-        keep, send, inverse = project(place, activations, cotangent)
+        keep, send, inverse = project(activations, cotangent)
         core_part = swap(send, "core")
-        *sent, own = merge(place, keep, core_part)
-        parts = [swap(part, QUAD, i, 4) for i, part in zip((1, 2, 3), sent)]
+        *sent, own = merge(keep, core_part)
+        parts = [swap(part, QUAD, i, 4) for i, part in zip((3, 1, 2), sent)]
 
     with jax.named_scope("deltas_over_islands"):
         local = lax.optimization_barrier((local_slab, own))[0]
@@ -204,7 +202,7 @@
         delta_y = swap(delta, "island", 3, islands)
 
     with jax.named_scope("projection_grad"):
-        combined = combine(place, own, parts, weight_z)
+        combined = combine(own, parts, weight_z)
         combined, delta_y = lax.optimization_barrier((combined, delta_y))
         chunks = lax.all_to_all(combined, "zh", 0, 0)
 
@@ -212,7 +210,7 @@
         later = lax.optimization_barrier((weight_z, delta))[0]
         w01 = swap(later, "xh")
         pieces = (weight_z, w01, swap(weight_z, "core"), swap(w01, "core"))
-        values = project_forward(place, activations, inverse, norm_gain, pieces)
+        values = project_forward(activations, inverse, norm_gain, pieces)
 
     with jax.named_scope("deltas_over_islands"):
         delta = delta + delta_y

time: 103 us -> 101 us (0.981)
  Pallas kernels: 8.57 us -> 6.24 us
    ppermute x10, waiting for transfers between devices: 6.3 us -> 5.11 us  [swap(): return lax.ppermute(value, axis, [(i, i ^ flip) for i in range(size)])]
  transfers between devices with their start and end apart: 13 -> 13, of which waited for: 5 -> 4; matrix products, arithmetic and copies ran while one was open for 3% -> 3% of each run, Pallas kernels for 8% -> 5%
where the time goes in v4:
time: 101 us; the launch traced here: 100 us
  starting transfers between devices  70.8 us (70%)
  waiting for transfers between devices  12.4 us (12%)
  local copies, waits for them, and re-layouts  7.95 us (8%)
  Pallas kernels  6.24 us (6%)
  other arithmetic  1.76 us (2%)
    ppermute x10, starting transfers between devices, swap(): return lax.ppermute(value, axis, [(i, i ^ flip) for i in range(size)])  34.4 us
    all_to_all x1, starting transfers between devices, shards(): weight_z = lax.all_to_all(spread(weight, depth * ZL), ('zh', 'zl'), 0, 0)  15.7 us
    all_to_all x1, starting transfers between devices, shards(): chunks = lax.all_to_all(combined, 'zh', 0, 0)  11.6 us
    all_to_all x1, starting transfers between devices, to_all(): lax.all_to_all(jnp.broadcast_to(value[None], (size,) + value.shape), axis...  9.07 us
    unnamed x19, local copies, waits for them, and re-layouts  6.7 us
    ppermute x10, waiting for transfers between devices, swap(): return lax.ppermute(value, axis, [(i, i ^ flip) for i in range(size)])  5.11 us
    all_to_all x1, waiting for transfers between devices, to_all(): lax.all_to_all(jnp.broadcast_to(value[None], (size,) + value.shape), axis...  3.98 us
    all_to_all x1, waiting for transfers between devices, shards(): chunks = lax.all_to_all(combined, 'zh', 0, 0)  3.28 us
  transfers between devices with their start and end apart: 13, of which 4 were waited for; matrix products, arithmetic and copies ran while one was open for 3% of the time, Pallas kernels for 5%

profile of v4, /device:TPU:1, one launch (start us, length us, event | category | flops | bytes accessed | tf_op | source)
XLA Modules:
  0.0 100.0 jit_solution(6385829879615045750)
XLA Ops:
  0.6 0.7 copy-done.4
  1.4 0.9 spread.1
  2.3 15.7 %all-to-all-start = ((bf16[16,128,128]{2,1,0:T(8,128)(2,1)}), bf16[16,128,128]{2,1,0:T(8,128)(2,1)S(1)}, u32[]{:S(2)}, u32[]{:S(2)}) async-start(bf16[16,128,128]{2,1,0:T(8,128)(2,1)} %spread.1), calls=%async_computation | async-start | bytes 1048576 | tf_op jit(solution)/shard_map/weight_over_z/all_to_all | solution.py:190
  18.0 2.2 %copy-done = bf16[256,8192]{1,0:T(8,128)(2,1)S(1)} copy-done((bf16[256,8192]{1,0:T(8,128)(2,1)S(1)}, bf16[256,8192]{1,0:T(8,128)(2,1)}, u32[]{:S(2)}) %copy-start) | copy-done | bytes 4194328
  20.2 0.8 copy-done.2
  21.1 1.7 %project.1 = (bf16[4,8,128,128]{3,2,1,0:T(8,128)(2,1)S(1)}, bf16[4,8,128,128]{3,2,1,0:T(8,128)(2,1)S(1)}, f32[256,1]{1,0:T(8,128)S(1)}) custom-call(bf16[256,8192]{1,0:T(8,128)(2,1)S(1)} %copy-done, bf16[256,128]{1,0:T(8,128)(2,1)S(1)} %copy-done.2), custom_call_target="tpu_custom_call" | custom-call | flops 536870912 | bytes 6291456 | tf_op jit(solution)/shard_map/projection_grad/project/pallas_call | solution.py:74
  22.7 2.9 %collective-permute-start = (bf16[4,8,128,128]{3,2,1,0:T(8,128)(2,1)S(1)}, bf16[4,8,128,128]{3,2,1,0:T(8,128)(2,1)S(1)}, u32[]{:S(2)}, u32[]{:S(2)}) collective-permute-start(bf16[4,8,128,128]{3,2,1,0:T(8,128)(2,1)S(1)} %get-tuple-element.20), channel_id=1, source_target_pairs={{0,1},{1,0},{2,3},{3,2},{4,5},{5,4},{6,7},{7,6},{8,9},{9,8},{10,11... | collective-permute-start | bytes 3145736 | tf_op jit(solution)/shard_map/projection_grad/ppermute | solution.py:21
  25.6 2.3 %collective-permute-done.core_part = bf16[4,8,128,128]{3,2,1,0:T(8,128)(2,1)S(1)} collective-permute-done((bf16[4,8,128,128]{3,2,1,0:T(8,128)(2,1)S(1)}, bf16[4,8,128,128]{3,2,1,0:T(8,128)(2,1)S(1)}, u32[]{:S(2)}, u32[]{:S(2)}) %collective-permute-start) | collective-permute-done | bytes 1048608 | tf_op jit(solution)/shard_map/projection_grad/ppermute | solution.py:21
  27.9 0.2 merge.1
  28.1 6.0 %collective-permute-start.1 = (bf16[8,128,128]{2,1,0:T(8,128)(2,1)S(1)}, bf16[8,128,128]{2,1,0:T(8,128)(2,1)S(1)}, u32[]{:S(2)}, u32[]{:S(2)}) collective-permute-start(bf16[8,128,128]{2,1,0:T(8,128)(2,1)S(1)} %get-tuple-element.22), channel_id=1, source_target_pairs={{0,6},{2,4},{4,2},{6,0},{1,7},{3,5},{5,3},{7,1},{8,14},{10,12},{12... | collective-permute-start | bytes 786440 | tf_op jit(solution)/shard_map/projection_grad/ppermute | solution.py:21
  34.1 2.1 %collective-permute-start.2 = (bf16[8,128,128]{2,1,0:T(8,128)(2,1)S(1)}, bf16[8,128,128]{2,1,0:T(8,128)(2,1)S(1)}, u32[]{:S(2)}, u32[]{:S(2)}) collective-permute-start(bf16[8,128,128]{2,1,0:T(8,128)(2,1)S(1)} %get-tuple-element.23), channel_id=1, source_target_pairs={{0,2},{2,0},{4,6},{6,4},{1,3},{3,1},{5,7},{7,5},{8,10},{10,8},{12,... | collective-permute-start | bytes 786440 | tf_op jit(solution)/shard_map/projection_grad/ppermute | solution.py:21
  36.3 2.0 %collective-permute-start.3 = (bf16[8,128,128]{2,1,0:T(8,128)(2,1)S(1)}, bf16[8,128,128]{2,1,0:T(8,128)(2,1)S(1)}, u32[]{:S(2)}, u32[]{:S(2)}) collective-permute-start(bf16[8,128,128]{2,1,0:T(8,128)(2,1)S(1)} %get-tuple-element.24), channel_id=1, source_target_pairs={{0,4},{2,6},{4,0},{6,2},{1,5},{3,7},{5,1},{7,3},{8,12},{10,14},{12... | collective-permute-start | bytes 786440 | tf_op jit(solution)/shard_map/projection_grad/ppermute | solution.py:21
  38.3 3.2 %collective-permute-start.4 = (f32[64,448]{1,0:T(8,128)S(1)}, f32[64,448]{1,0:T(8,128)S(1)}, u32[]{:S(2)}, u32[]{:S(2)}) collective-permute-start(f32[64,448]{1,0:T(8,128)S(1)} %fusion.1), channel_id=1, source_target_pairs={{0,64},{64,0},{128,192},{192,128},{256,320},{320,256},{384,448},{4... | collective-permute-start | bytes 344072 | tf_op jit(solution)/shard_map/deltas_over_islands/ppermute | solution.py:21
  41.5 2.8 %collective-permute-done.4 = f32[64,448]{1,0:T(8,128)S(1)} collective-permute-done((f32[64,448]{1,0:T(8,128)S(1)}, f32[64,448]{1,0:T(8,128)S(1)}, u32[]{:S(2)}, u32[]{:S(2)}) %collective-permute-start.4) | collective-permute-done | bytes 114720 | tf_op jit(solution)/shard_map/deltas_over_islands/ppermute | solution.py:21
  44.3 4.6 %collective-permute-start.5 = (f32[64,448]{1,0:T(8,128)S(1)}, f32[64,448]{1,0:T(8,128)}, u32[]{:S(2)}, u32[]{:S(2)}) collective-permute-start(f32[64,448]{1,0:T(8,128)S(1)} %add.31), channel_id=1, source_target_pairs={{0,192},{64,128},{128,64},{192,0},{256,448},{320,384},{384,320},{4... | collective-permute-start | bytes 344072 | tf_op jit(solution)/shard_map/deltas_over_islands/ppermute | solution.py:21
  49.0 4.6 %collective-permute-start.6 = (bf16[16,128,128]{2,1,0:T(8,128)(2,1)S(1)}, bf16[16,128,128]{2,1,0:T(8,128)(2,1)S(1)}, u32[]{:S(2)}, u32[]{:S(2)}) collective-permute-start(bf16[16,128,128]{2,1,0:T(8,128)(2,1)S(1)} %all-to-all-done.weight.w00), channel_id=1, source_target_pairs={{0,2},{2,0},{1,3},{3,1},{4,6},{6,4},{5,7},{7,5},{8,10},{10,8},{9,1... | collective-permute-start | bytes 1572872 | tf_op jit(solution)/shard_map/values/ppermute | solution.py:21
  53.6 0.0 collective-permute-done.3.three
  53.6 0.9 combine.1
  54.6 11.6 %all-to-all-start.1 = ((bf16[8,144,128]{2,1,0:T(8,128)(2,1)}), bf16[8,144,128]{2,1,0:T(8,128)(2,1)S(1)}, u32[]{:S(2)}, u32[]{:S(2)}) async-start(bf16[8,144,128]{2,1,0:T(8,128)(2,1)} %combine.1), calls=%async_computation.1 | async-start | bytes 589824 | tf_op jit(solution)/shard_map/projection_grad/all_to_all | solution.py:207
  66.2 4.8 %collective-permute-start.7 = (bf16[16,128,128]{2,1,0:T(8,128)(2,1)S(1)}, bf16[16,128,128]{2,1,0:T(8,128)(2,1)S(1)}, u32[]{:S(2)}, u32[]{:S(2)}) collective-permute-start(bf16[16,128,128]{2,1,0:T(8,128)(2,1)S(1)} %all-to-all-done.weight.w00), channel_id=1, source_target_pairs={{0,1},{1,0},{2,3},{3,2},{4,5},{5,4},{6,7},{7,6},{8,9},{9,8},{10,11... | collective-permute-start | bytes 1572872 | tf_op jit(solution)/shard_map/values/ppermute | solution.py:21
  71.0 1.9 %collective-permute-start.8 = (bf16[16,128,128]{2,1,0:T(8,128)(2,1)S(1)}, bf16[16,128,128]{2,1,0:T(8,128)(2,1)S(1)}, u32[]{:S(2)}, u32[]{:S(2)}) collective-permute-start(bf16[16,128,128]{2,1,0:T(8,128)(2,1)S(1)} %collective-permute-done.6.w01), channel_id=1, source_target_pairs={{0,1},{1,0},{2,3},{3,2},{4,5},{5,4},{6,7},{7,6},{8,9},{9,8},{10,11... | collective-permute-start | bytes 1572872 | tf_op jit(solution)/shard_map/values/ppermute | solution.py:21
  72.9 0.9 add.37
  73.9 2.2 %collective-permute-start.9 = (f32[64,448]{1,0:T(8,128)S(1)}, f32[64,448]{1,0:T(8,128)S(1)}, u32[]{:S(2)}, u32[]{:S(2)}) collective-permute-start(f32[64,448]{1,0:T(8,128)S(1)} %add.37), channel_id=1, source_target_pairs={{0,256},{64,320},{128,384},{192,448},{256,0},{320,64},{384,128},{4... | collective-permute-start | bytes 344072 | tf_op jit(solution)/shard_map/deltas_over_islands/ppermute | solution.py:21
  76.1 2.2 %copy-done.1 = bf16[256,8192]{1,0:T(8,128)(2,1)S(1)} copy-done((bf16[256,8192]{1,0:T(8,128)(2,1)S(1)}, bf16[256,8192]{1,0:T(8,128)(2,1)}, u32[]{:S(2)}) %copy-start.1) | copy-done | bytes 4194328
  78.3 2.5 %project_forward.1 = bf16[256,128]{1,0:T(8,128)(2,1)} custom-call(bf16[256,8192]{1,0:T(8,128)(2,1)S(1)} %copy-done.1, f32[256,1]{1,0:T(8,128)S(1)} %get-tuple-element.27.inverse, f32[64,128]{1,0:T(8,128)S(1)} %bitcast.14, bf16[16,128,128]{2,1,0:T(8,128)(2,1)S(1)} %all-to-all-done.weight.w00, bf16[16,128,128]{2,1,0:T(8,128)(2,1)S(1)} %collective-permute-done.6.w01, ...), custom_call_target="tpu_custom_call" | custom-call | flops 536870912 | bytes 6291456 | tf_op jit(solution)/shard_map/values/project_forward/pallas_call | solution.py:172
  80.8 3.3 %all-to-all-done.1 = bf16[8,144,128]{2,1,0:T(8,128)(2,1)S(1)} async-done(((bf16[8,144,128]{2,1,0:T(8,128)(2,1)}), bf16[8,144,128]{2,1,0:T(8,128)(2,1)S(1)}, u32[]{:S(2)}, u32[]{:S(2)}) %all-to-all-start.1) | async-done | bytes 294944 | tf_op jit(solution)/shard_map/projection_grad/all_to_all | solution.py:207
  84.2 0.6 broadcast_in_dim.10
  84.8 9.1 %all-to-all-start.2 = ((f32[8,8,128]{2,1,0:T(8,128)}), f32[8,8,128]{2,1,0:T(8,128)S(1)}, u32[]{:S(2)}, u32[]{:S(2)}) async-start(f32[8,8,128]{2,1,0:T(8,128)} %broadcast_in_dim.10), calls=%async_computation.2 | async-start | bytes 65536 | tf_op jit(solution)/shard_map/gain_grad/all_to_all | solution.py:25
  93.9 0.7 multiply_subtract_fusion
  94.7 0.7 copy.14
  95.4 4.0 %all-to-all-done.2 = f32[8,8,128]{2,1,0:T(8,128)S(1)} async-done(((f32[8,8,128]{2,1,0:T(8,128)}), f32[8,8,128]{2,1,0:T(8,128)S(1)}, u32[]{:S(2)}, u32[]{:S(2)}) %all-to-all-start.2) | async-done | bytes 32800 | tf_op jit(solution)/shard_map/gain_grad/all_to_all | solution.py:25
  99.4 0.6 copy.13
  (29 shorter events, 0.2 us)
Async XLA Ops:
  0.6 0.8 copy-start.4
  1.4 36.9 %copy-start.5 = (f32[64,448]{1,0:T(8,128)S(1)}, f32[64,448]{1,0:T(8,128)}, u32[]{:S(2)}) copy-start(f32[64,448]{1,0:T(8,128)} %param.11) | copy-start | bytes 344068
  1.4 36.9 %copy-start.8 = (bf16[1,64,448]{2,1,0:T(8,128)(2,1)S(1)}, bf16[1,64,448]{2,1,0:T(8,128)(2,1)}, u32[]{:S(2)}) copy-start(bf16[1,64,448]{2,1,0:T(8,128)(2,1)} %param.12) | copy-start | bytes 172036
  2.3 46.7 %all-to-all-start = ((bf16[16,128,128]{2,1,0:T(8,128)(2,1)}), bf16[16,128,128]{2,1,0:T(8,128)(2,1)S(1)}, u32[]{:S(2)}, u32[]{:S(2)}) async-start(bf16[16,128,128]{2,1,0:T(8,128)(2,1)} %spread.1), calls=%async_computation | async-start | bytes 1048576 | tf_op jit(solution)/shard_map/weight_over_z/all_to_all | solution.py:190
  18.0 2.2 %copy-start = (bf16[256,8192]{1,0:T(8,128)(2,1)S(1)}, bf16[256,8192]{1,0:T(8,128)(2,1)}, u32[]{:S(2)}) copy-start(bf16[256,8192]{1,0:T(8,128)(2,1)} %x.3) | copy-start | bytes 12582916
  20.2 0.8 copy-start.2
  21.1 51.9 %copy-start.3 = (f32[1,8192]{1,0:T(1,128)S(1)}, f32[1,8192]{1,0:T(1,128)}, u32[]{:S(2)}) copy-start(f32[1,8192]{1,0:T(1,128)} %param.9) | copy-start | bytes 98308
  22.7 5.1 %collective-permute-start = (bf16[4,8,128,128]{3,2,1,0:T(8,128)(2,1)S(1)}, bf16[4,8,128,128]{3,2,1,0:T(8,128)(2,1)S(1)}, u32[]{:S(2)}, u32[]{:S(2)}) collective-permute-start(bf16[4,8,128,128]{3,2,1,0:T(8,128)(2,1)S(1)} %get-tuple-element.20), channel_id=1, source_target_pairs={{0,1},{1,0},{2,3},{3,2},{4,5},{5,4},{6,7},{7,6},{8,9},{9,8},{10,11... | collective-permute-start | bytes 3145736 | tf_op jit(solution)/shard_map/projection_grad/ppermute | solution.py:21
  28.1 25.5 %collective-permute-start.1 = (bf16[8,128,128]{2,1,0:T(8,128)(2,1)S(1)}, bf16[8,128,128]{2,1,0:T(8,128)(2,1)S(1)}, u32[]{:S(2)}, u32[]{:S(2)}) collective-permute-start(bf16[8,128,128]{2,1,0:T(8,128)(2,1)S(1)} %get-tuple-element.22), channel_id=1, source_target_pairs={{0,6},{2,4},{4,2},{6,0},{1,7},{3,5},{5,3},{7,1},{8,14},{10,12},{12... | collective-permute-start | bytes 786440 | tf_op jit(solution)/shard_map/projection_grad/ppermute | solution.py:21
  34.1 19.5 %collective-permute-start.2 = (bf16[8,128,128]{2,1,0:T(8,128)(2,1)S(1)}, bf16[8,128,128]{2,1,0:T(8,128)(2,1)S(1)}, u32[]{:S(2)}, u32[]{:S(2)}) collective-permute-start(bf16[8,128,128]{2,1,0:T(8,128)(2,1)S(1)} %get-tuple-element.23), channel_id=1, source_target_pairs={{0,2},{2,0},{4,6},{6,4},{1,3},{3,1},{5,7},{7,5},{8,10},{10,8},{12,... | collective-permute-start | bytes 786440 | tf_op jit(solution)/shard_map/projection_grad/ppermute | solution.py:21
  36.3 17.4 %collective-permute-start.3 = (bf16[8,128,128]{2,1,0:T(8,128)(2,1)S(1)}, bf16[8,128,128]{2,1,0:T(8,128)(2,1)S(1)}, u32[]{:S(2)}, u32[]{:S(2)}) collective-permute-start(bf16[8,128,128]{2,1,0:T(8,128)(2,1)S(1)} %get-tuple-element.24), channel_id=1, source_target_pairs={{0,4},{2,6},{4,0},{6,2},{1,5},{3,7},{5,1},{7,3},{8,12},{10,14},{12... | collective-permute-start | bytes 786440 | tf_op jit(solution)/shard_map/projection_grad/ppermute | solution.py:21
  38.3 6.0 %collective-permute-start.4 = (f32[64,448]{1,0:T(8,128)S(1)}, f32[64,448]{1,0:T(8,128)S(1)}, u32[]{:S(2)}, u32[]{:S(2)}) collective-permute-start(f32[64,448]{1,0:T(8,128)S(1)} %fusion.1), channel_id=1, source_target_pairs={{0,64},{64,0},{128,192},{192,128},{256,320},{320,256},{384,448},{4... | collective-permute-start | bytes 344072 | tf_op jit(solution)/shard_map/deltas_over_islands/ppermute | solution.py:21
  44.3 10.3 %collective-permute-start.5 = (f32[64,448]{1,0:T(8,128)S(1)}, f32[64,448]{1,0:T(8,128)}, u32[]{:S(2)}, u32[]{:S(2)}) collective-permute-start(f32[64,448]{1,0:T(8,128)S(1)} %add.31), channel_id=1, source_target_pairs={{0,192},{64,128},{128,64},{192,0},{256,448},{320,384},{384,320},{4... | collective-permute-start | bytes 344072 | tf_op jit(solution)/shard_map/deltas_over_islands/ppermute | solution.py:21
  49.0 22.0 %collective-permute-start.6 = (bf16[16,128,128]{2,1,0:T(8,128)(2,1)S(1)}, bf16[16,128,128]{2,1,0:T(8,128)(2,1)S(1)}, u32[]{:S(2)}, u32[]{:S(2)}) collective-permute-start(bf16[16,128,128]{2,1,0:T(8,128)(2,1)S(1)} %all-to-all-done.weight.w00), channel_id=1, source_target_pairs={{0,2},{2,0},{1,3},{3,1},{4,6},{6,4},{5,7},{7,5},{8,10},{10,8},{9,1... | collective-permute-start | bytes 1572872 | tf_op jit(solution)/shard_map/values/ppermute | solution.py:21
  54.6 39.3 %copy-start.6 = (f32[64,448]{1,0:T(8,128)S(1)}, f32[64,448]{1,0:T(8,128)}, u32[]{:S(2)}) copy-start(f32[64,448]{1,0:T(8,128)} %param.11) | copy-start | bytes 344068
  54.6 39.3 %copy-start.7 = (f32[64,448]{1,0:T(8,128)S(1)}, f32[64,448]{1,0:T(8,128)}, u32[]{:S(2)}) copy-start(f32[64,448]{1,0:T(8,128)} %param.13) | copy-start | bytes 344068
  54.6 29.5 %all-to-all-start.1 = ((bf16[8,144,128]{2,1,0:T(8,128)(2,1)}), bf16[8,144,128]{2,1,0:T(8,128)(2,1)S(1)}, u32[]{:S(2)}, u32[]{:S(2)}) async-start(bf16[8,144,128]{2,1,0:T(8,128)(2,1)} %combine.1), calls=%async_computation.1 | async-start | bytes 589824 | tf_op jit(solution)/shard_map/projection_grad/all_to_all | solution.py:207
  66.2 9.9 %collective-permute-start.7 = (bf16[16,128,128]{2,1,0:T(8,128)(2,1)S(1)}, bf16[16,128,128]{2,1,0:T(8,128)(2,1)S(1)}, u32[]{:S(2)}, u32[]{:S(2)}) collective-permute-start(bf16[16,128,128]{2,1,0:T(8,128)(2,1)S(1)} %all-to-all-done.weight.w00), channel_id=1, source_target_pairs={{0,1},{1,0},{2,3},{3,2},{4,5},{5,4},{6,7},{7,6},{8,9},{9,8},{10,11... | collective-permute-start | bytes 1572872 | tf_op jit(solution)/shard_map/values/ppermute | solution.py:21
  71.0 5.1 %collective-permute-start.8 = (bf16[16,128,128]{2,1,0:T(8,128)(2,1)S(1)}, bf16[16,128,128]{2,1,0:T(8,128)(2,1)S(1)}, u32[]{:S(2)}, u32[]{:S(2)}) collective-permute-start(bf16[16,128,128]{2,1,0:T(8,128)(2,1)S(1)} %collective-permute-done.6.w01), channel_id=1, source_target_pairs={{0,1},{1,0},{2,3},{3,2},{4,5},{5,4},{6,7},{7,6},{8,9},{9,8},{10,11... | collective-permute-start | bytes 1572872 | tf_op jit(solution)/shard_map/values/ppermute | solution.py:21
  73.9 20.0 %collective-permute-start.9 = (f32[64,448]{1,0:T(8,128)S(1)}, f32[64,448]{1,0:T(8,128)S(1)}, u32[]{:S(2)}, u32[]{:S(2)}) collective-permute-start(f32[64,448]{1,0:T(8,128)S(1)} %add.37), channel_id=1, source_target_pairs={{0,256},{64,320},{128,384},{192,448},{256,0},{320,64},{384,128},{4... | collective-permute-start | bytes 344072 | tf_op jit(solution)/shard_map/deltas_over_islands/ppermute | solution.py:21
  76.1 2.2 %copy-start.1 = (bf16[256,8192]{1,0:T(8,128)(2,1)S(1)}, bf16[256,8192]{1,0:T(8,128)(2,1)}, u32[]{:S(2)}) copy-start(bf16[256,8192]{1,0:T(8,128)(2,1)} %x.3) | copy-start | bytes 12582916
  84.8 14.6 %all-to-all-start.2 = ((f32[8,8,128]{2,1,0:T(8,128)}), f32[8,8,128]{2,1,0:T(8,128)S(1)}, u32[]{:S(2)}, u32[]{:S(2)}) async-start(f32[8,8,128]{2,1,0:T(8,128)} %broadcast_in_dim.10), calls=%async_computation.2 | async-start | bytes 65536 | tf_op jit(solution)/shard_map/gain_grad/all_to_all | solution.py:25

commit v5 on v4

--- a/solution.py
+++ b/solution.py
@@ -15,6 +15,7 @@
 f32, bf16 = jnp.float32, jnp.bfloat16
 VMEM = pl.BlockSpec(memory_space=pltpu.VMEM)
 SMALL = 20 * 2**20
+LIMIT = 60 * 2**20
 
 
 def swap(value, axis, flip=1, size=2):
@@ -29,18 +30,24 @@
     return pl.BlockSpec(shape, lambda *_: (0,) * len(shape))
 
 
-def spread_kernel(value, out):
-    for i in range(out.shape[0]):
-        out[i] = value[0]
+def spread_kernel(value, out, sems):
+    copies = [
+        pltpu.make_async_copy(value.at[0], out.at[i], sems.at[i]) for i in range(out.shape[0])
+    ]
+    for copy in copies:
+        copy.start()
+    for copy in copies:
+        copy.wait()
 
 
 def spread(value, size):
     return pl.pallas_call(
         spread_kernel,
         out_shape=jax.ShapeDtypeStruct((size,) + value.shape[1:], value.dtype),
-        in_specs=[VMEM],
-        out_specs=VMEM,
-        compiler_params=pltpu.CompilerParams(vmem_limit_bytes=SMALL),
+        in_specs=[pl.BlockSpec(memory_space=pl.ANY)],
+        out_specs=pl.BlockSpec(memory_space=pl.ANY),
+        scratch_shapes=[pltpu.SemaphoreType.DMA((size,))],
+        compiler_params=pltpu.CompilerParams(vmem_limit_bytes=LIMIT),
         name="spread",
     )(value)
 

time: 101 us -> 116 us (1.15)
  Pallas kernels: 6.24 us -> 22.5 us
    pallas_call x1, Pallas kernels: 0.88 us -> 17.1 us  [spread(): pl.pallas_call(spread_kernel, out_shape=jax.ShapeDtypeStruct((size,) + va...]
    unnamed x19 -> x17, local copies, waits for them, and re-layouts: 6.7 us -> 5.96 us
where the time goes in v5:
time: 116 us
  starting transfers between devices  70.7 us (61%)
  Pallas kernels  22.5 us (19%)
  waiting for transfers between devices  12.4 us (11%)
  local copies, waits for them, and re-layouts  7.2 us (6%)
  other arithmetic  1.76 us (2%)
    ppermute x10, starting transfers between devices, swap(): return lax.ppermute(value, axis, [(i, i ^ flip) for i in range(size)])  34.4 us
    pallas_call x1, Pallas kernels, spread(): pl.pallas_call(spread_kernel, out_shape=jax.ShapeDtypeStruct((size,) + va...  17.1 us
    all_to_all x1, starting transfers between devices, shards(): weight_z = lax.all_to_all(spread(weight, depth * ZL), ('zh', 'zl'), 0, 0)  15.8 us
    all_to_all x1, starting transfers between devices, shards(): chunks = lax.all_to_all(combined, 'zh', 0, 0)  11.6 us
    all_to_all x1, starting transfers between devices, to_all(): lax.all_to_all(jnp.broadcast_to(value[None], (size,) + value.shape), axis...  9.05 us
    unnamed x17, local copies, waits for them, and re-layouts  5.96 us
    ppermute x10, waiting for transfers between devices, swap(): return lax.ppermute(value, axis, [(i, i ^ flip) for i in range(size)])  5.12 us
    all_to_all x1, waiting for transfers between devices, to_all(): lax.all_to_all(jnp.broadcast_to(value[None], (size,) + value.shape), axis...  3.98 us
  transfers between devices with their start and end apart: 13, of which 4 were waited for; matrix products, arithmetic and copies ran while one was open for 3% of the time, Pallas kernels for 5%

profile of v5, /device:TPU:1, one launch (start us, length us, event | category | flops | bytes accessed | tf_op | source)
XLA Modules:
  0.0 115.5 jit_solution(8563907188276875113)
XLA Ops:
  0.6 0.0 copy-start.4
  0.7 17.1 %spread.1 = bf16[16,128,128]{2,1,0:T(8,128)(2,1)} custom-call(bf16[1,128,128]{2,1,0:T(8,128)(2,1)} %value.1), custom_call_target="tpu_custom_call" | custom-call | tf_op jit(solution)/shard_map/weight_over_z/spread/pallas_call | solution.py:44
  17.8 15.8 %all-to-all-start = ((bf16[16,128,128]{2,1,0:T(8,128)(2,1)}), bf16[16,128,128]{2,1,0:T(8,128)(2,1)S(1)}, u32[]{:S(2)}, u32[]{:S(2)}) async-start(bf16[16,128,128]{2,1,0:T(8,128)(2,1)} %spread.1), calls=%async_computation | async-start | bytes 1048576 | tf_op jit(solution)/shard_map/weight_over_z/all_to_all | solution.py:197
  33.6 2.2 %copy-done = bf16[256,8192]{1,0:T(8,128)(2,1)S(1)} copy-done((bf16[256,8192]{1,0:T(8,128)(2,1)S(1)}, bf16[256,8192]{1,0:T(8,128)(2,1)}, u32[]{:S(2)}) %copy-start) | copy-done | bytes 4194328
  35.7 0.8 copy-done.2
  36.6 1.7 %project.1 = (bf16[4,8,128,128]{3,2,1,0:T(8,128)(2,1)S(1)}, bf16[4,8,128,128]{3,2,1,0:T(8,128)(2,1)S(1)}, f32[256,1]{1,0:T(8,128)S(1)}) custom-call(bf16[256,8192]{1,0:T(8,128)(2,1)S(1)} %copy-done, bf16[256,128]{1,0:T(8,128)(2,1)S(1)} %copy-done.2), custom_call_target="tpu_custom_call" | custom-call | flops 536870912 | bytes 6291456 | tf_op jit(solution)/shard_map/projection_grad/project/pallas_call | solution.py:81
  38.3 2.9 %collective-permute-start = (bf16[4,8,128,128]{3,2,1,0:T(8,128)(2,1)S(1)}, bf16[4,8,128,128]{3,2,1,0:T(8,128)(2,1)S(1)}, u32[]{:S(2)}, u32[]{:S(2)}) collective-permute-start(bf16[4,8,128,128]{3,2,1,0:T(8,128)(2,1)S(1)} %get-tuple-element.20), channel_id=1, source_target_pairs={{0,1},{1,0},{2,3},{3,2},{4,5},{5,4},{6,7},{7,6},{8,9},{9,8},{10,11... | collective-permute-start | bytes 3145736 | tf_op jit(solution)/shard_map/projection_grad/ppermute | solution.py:22
  41.1 2.3 %collective-permute-done.core_part = bf16[4,8,128,128]{3,2,1,0:T(8,128)(2,1)S(1)} collective-permute-done((bf16[4,8,128,128]{3,2,1,0:T(8,128)(2,1)S(1)}, bf16[4,8,128,128]{3,2,1,0:T(8,128)(2,1)S(1)}, u32[]{:S(2)}, u32[]{:S(2)}) %collective-permute-start) | collective-permute-done | bytes 1048608 | tf_op jit(solution)/shard_map/projection_grad/ppermute | solution.py:22
  43.4 0.2 merge.1
  43.6 6.0 %collective-permute-start.1 = (bf16[8,128,128]{2,1,0:T(8,128)(2,1)S(1)}, bf16[8,128,128]{2,1,0:T(8,128)(2,1)S(1)}, u32[]{:S(2)}, u32[]{:S(2)}) collective-permute-start(bf16[8,128,128]{2,1,0:T(8,128)(2,1)S(1)} %get-tuple-element.22), channel_id=1, source_target_pairs={{0,6},{2,4},{4,2},{6,0},{1,7},{3,5},{5,3},{7,1},{8,14},{10,12},{12... | collective-permute-start | bytes 786440 | tf_op jit(solution)/shard_map/projection_grad/ppermute | solution.py:22
  49.6 2.1 %collective-permute-start.2 = (bf16[8,128,128]{2,1,0:T(8,128)(2,1)S(1)}, bf16[8,128,128]{2,1,0:T(8,128)(2,1)S(1)}, u32[]{:S(2)}, u32[]{:S(2)}) collective-permute-start(bf16[8,128,128]{2,1,0:T(8,128)(2,1)S(1)} %get-tuple-element.23), channel_id=1, source_target_pairs={{0,2},{2,0},{4,6},{6,4},{1,3},{3,1},{5,7},{7,5},{8,10},{10,8},{12,... | collective-permute-start | bytes 786440 | tf_op jit(solution)/shard_map/projection_grad/ppermute | solution.py:22
  51.8 2.0 %collective-permute-start.3 = (bf16[8,128,128]{2,1,0:T(8,128)(2,1)S(1)}, bf16[8,128,128]{2,1,0:T(8,128)(2,1)S(1)}, u32[]{:S(2)}, u32[]{:S(2)}) collective-permute-start(bf16[8,128,128]{2,1,0:T(8,128)(2,1)S(1)} %get-tuple-element.24), channel_id=1, source_target_pairs={{0,4},{2,6},{4,0},{6,2},{1,5},{3,7},{5,1},{7,3},{8,12},{10,14},{12... | collective-permute-start | bytes 786440 | tf_op jit(solution)/shard_map/projection_grad/ppermute | solution.py:22
  53.8 3.2 %collective-permute-start.4 = (f32[64,448]{1,0:T(8,128)S(1)}, f32[64,448]{1,0:T(8,128)S(1)}, u32[]{:S(2)}, u32[]{:S(2)}) collective-permute-start(f32[64,448]{1,0:T(8,128)S(1)} %fusion.1), channel_id=1, source_target_pairs={{0,64},{64,0},{128,192},{192,128},{256,320},{320,256},{384,448},{4... | collective-permute-start | bytes 344072 | tf_op jit(solution)/shard_map/deltas_over_islands/ppermute | solution.py:22
  57.0 2.8 %collective-permute-done.4 = f32[64,448]{1,0:T(8,128)S(1)} collective-permute-done((f32[64,448]{1,0:T(8,128)S(1)}, f32[64,448]{1,0:T(8,128)S(1)}, u32[]{:S(2)}, u32[]{:S(2)}) %collective-permute-start.4) | collective-permute-done | bytes 114720 | tf_op jit(solution)/shard_map/deltas_over_islands/ppermute | solution.py:22
  59.8 4.6 %collective-permute-start.5 = (f32[64,448]{1,0:T(8,128)S(1)}, f32[64,448]{1,0:T(8,128)}, u32[]{:S(2)}, u32[]{:S(2)}) collective-permute-start(f32[64,448]{1,0:T(8,128)S(1)} %add.31), channel_id=1, source_target_pairs={{0,192},{64,128},{128,64},{192,0},{256,448},{320,384},{384,320},{4... | collective-permute-start | bytes 344072 | tf_op jit(solution)/shard_map/deltas_over_islands/ppermute | solution.py:22
  64.5 4.6 %collective-permute-start.6 = (bf16[16,128,128]{2,1,0:T(8,128)(2,1)S(1)}, bf16[16,128,128]{2,1,0:T(8,128)(2,1)S(1)}, u32[]{:S(2)}, u32[]{:S(2)}) collective-permute-start(bf16[16,128,128]{2,1,0:T(8,128)(2,1)S(1)} %all-to-all-done.weight.w00), channel_id=1, source_target_pairs={{0,2},{2,0},{1,3},{3,1},{4,6},{6,4},{5,7},{7,5},{8,10},{10,8},{9,1... | collective-permute-start | bytes 1572872 | tf_op jit(solution)/shard_map/values/ppermute | solution.py:22
  69.1 0.0 collective-permute-done.3.three
  69.2 0.9 combine.1
  70.1 11.6 %all-to-all-start.1 = ((bf16[8,144,128]{2,1,0:T(8,128)(2,1)}), bf16[8,144,128]{2,1,0:T(8,128)(2,1)S(1)}, u32[]{:S(2)}, u32[]{:S(2)}) async-start(bf16[8,144,128]{2,1,0:T(8,128)(2,1)} %combine.1), calls=%async_computation.1 | async-start | bytes 589824 | tf_op jit(solution)/shard_map/projection_grad/all_to_all | solution.py:214
  81.7 4.8 %collective-permute-start.7 = (bf16[16,128,128]{2,1,0:T(8,128)(2,1)S(1)}, bf16[16,128,128]{2,1,0:T(8,128)(2,1)S(1)}, u32[]{:S(2)}, u32[]{:S(2)}) collective-permute-start(bf16[16,128,128]{2,1,0:T(8,128)(2,1)S(1)} %all-to-all-done.weight.w00), channel_id=1, source_target_pairs={{0,1},{1,0},{2,3},{3,2},{4,5},{5,4},{6,7},{7,6},{8,9},{9,8},{10,11... | collective-permute-start | bytes 1572872 | tf_op jit(solution)/shard_map/values/ppermute | solution.py:22
  86.5 1.9 %collective-permute-start.8 = (bf16[16,128,128]{2,1,0:T(8,128)(2,1)S(1)}, bf16[16,128,128]{2,1,0:T(8,128)(2,1)S(1)}, u32[]{:S(2)}, u32[]{:S(2)}) collective-permute-start(bf16[16,128,128]{2,1,0:T(8,128)(2,1)S(1)} %collective-permute-done.6.w01), channel_id=1, source_target_pairs={{0,1},{1,0},{2,3},{3,2},{4,5},{5,4},{6,7},{7,6},{8,9},{9,8},{10,11... | collective-permute-start | bytes 1572872 | tf_op jit(solution)/shard_map/values/ppermute | solution.py:22
  88.5 0.9 add.37
  89.4 2.2 %collective-permute-start.9 = (f32[64,448]{1,0:T(8,128)S(1)}, f32[64,448]{1,0:T(8,128)S(1)}, u32[]{:S(2)}, u32[]{:S(2)}) collective-permute-start(f32[64,448]{1,0:T(8,128)S(1)} %add.37), channel_id=1, source_target_pairs={{0,256},{64,320},{128,384},{192,448},{256,0},{320,64},{384,128},{4... | collective-permute-start | bytes 344072 | tf_op jit(solution)/shard_map/deltas_over_islands/ppermute | solution.py:22
  91.6 2.2 %copy-done.1 = bf16[256,8192]{1,0:T(8,128)(2,1)S(1)} copy-done((bf16[256,8192]{1,0:T(8,128)(2,1)S(1)}, bf16[256,8192]{1,0:T(8,128)(2,1)}, u32[]{:S(2)}) %copy-start.1) | copy-done | bytes 4194328
  93.8 2.5 %project_forward.1 = bf16[256,128]{1,0:T(8,128)(2,1)} custom-call(bf16[256,8192]{1,0:T(8,128)(2,1)S(1)} %copy-done.1, f32[256,1]{1,0:T(8,128)S(1)} %get-tuple-element.27.inverse, f32[64,128]{1,0:T(8,128)S(1)} %bitcast.14, bf16[16,128,128]{2,1,0:T(8,128)(2,1)S(1)} %all-to-all-done.weight.w00, bf16[16,128,128]{2,1,0:T(8,128)(2,1)S(1)} %collective-permute-done.6.w01, ...), custom_call_target="tpu_custom_call" | custom-call | flops 536870912 | bytes 6291456 | tf_op jit(solution)/shard_map/values/project_forward/pallas_call | solution.py:179
  96.4 3.3 %all-to-all-done.1 = bf16[8,144,128]{2,1,0:T(8,128)(2,1)S(1)} async-done(((bf16[8,144,128]{2,1,0:T(8,128)(2,1)}), bf16[8,144,128]{2,1,0:T(8,128)(2,1)S(1)}, u32[]{:S(2)}, u32[]{:S(2)}) %all-to-all-start.1) | async-done | bytes 294944 | tf_op jit(solution)/shard_map/projection_grad/all_to_all | solution.py:214
  99.7 0.6 broadcast_in_dim.10
  100.3 9.1 %all-to-all-start.2 = ((f32[8,8,128]{2,1,0:T(8,128)}), f32[8,8,128]{2,1,0:T(8,128)S(1)}, u32[]{:S(2)}, u32[]{:S(2)}) async-start(f32[8,8,128]{2,1,0:T(8,128)} %broadcast_in_dim.10), calls=%async_computation.2 | async-start | bytes 65536 | tf_op jit(solution)/shard_map/gain_grad/all_to_all | solution.py:26
  109.4 0.7 multiply_subtract_fusion
  110.2 0.7 copy.14
  110.9 4.0 %all-to-all-done.2 = f32[8,8,128]{2,1,0:T(8,128)S(1)} async-done(((f32[8,8,128]{2,1,0:T(8,128)}), f32[8,8,128]{2,1,0:T(8,128)S(1)}, u32[]{:S(2)}, u32[]{:S(2)}) %all-to-all-start.2) | async-done | bytes 32800 | tf_op jit(solution)/shard_map/gain_grad/all_to_all | solution.py:26
  114.9 0.6 copy.13
  (27 shorter events, 0.2 us)
Async XLA Ops:
  0.6 53.1 %copy-start.7 = (bf16[1,64,448]{2,1,0:T(8,128)(2,1)S(1)}, bf16[1,64,448]{2,1,0:T(8,128)(2,1)}, u32[]{:S(2)}) copy-start(bf16[1,64,448]{2,1,0:T(8,128)(2,1)} %param.12) | copy-start | bytes 172036
  0.6 53.1 %copy-start.4 = (f32[64,448]{1,0:T(8,128)S(1)}, f32[64,448]{1,0:T(8,128)}, u32[]{:S(2)}) copy-start(f32[64,448]{1,0:T(8,128)} %param.11) | copy-start | bytes 344068
  17.8 46.7 %all-to-all-start = ((bf16[16,128,128]{2,1,0:T(8,128)(2,1)}), bf16[16,128,128]{2,1,0:T(8,128)(2,1)S(1)}, u32[]{:S(2)}, u32[]{:S(2)}) async-start(bf16[16,128,128]{2,1,0:T(8,128)(2,1)} %spread.1), calls=%async_computation | async-start | bytes 1048576 | tf_op jit(solution)/shard_map/weight_over_z/all_to_all | solution.py:197
  33.6 2.2 %copy-start = (bf16[256,8192]{1,0:T(8,128)(2,1)S(1)}, bf16[256,8192]{1,0:T(8,128)(2,1)}, u32[]{:S(2)}) copy-start(bf16[256,8192]{1,0:T(8,128)(2,1)} %x.3) | copy-start | bytes 12582916
  35.7 0.8 copy-start.2
  36.6 51.9 %copy-start.3 = (f32[1,8192]{1,0:T(1,128)S(1)}, f32[1,8192]{1,0:T(1,128)}, u32[]{:S(2)}) copy-start(f32[1,8192]{1,0:T(1,128)} %param.9) | copy-start | bytes 98308
  38.3 5.1 %collective-permute-start = (bf16[4,8,128,128]{3,2,1,0:T(8,128)(2,1)S(1)}, bf16[4,8,128,128]{3,2,1,0:T(8,128)(2,1)S(1)}, u32[]{:S(2)}, u32[]{:S(2)}) collective-permute-start(bf16[4,8,128,128]{3,2,1,0:T(8,128)(2,1)S(1)} %get-tuple-element.20), channel_id=1, source_target_pairs={{0,1},{1,0},{2,3},{3,2},{4,5},{5,4},{6,7},{7,6},{8,9},{9,8},{10,11... | collective-permute-start | bytes 3145736 | tf_op jit(solution)/shard_map/projection_grad/ppermute | solution.py:22
  43.6 25.5 %collective-permute-start.1 = (bf16[8,128,128]{2,1,0:T(8,128)(2,1)S(1)}, bf16[8,128,128]{2,1,0:T(8,128)(2,1)S(1)}, u32[]{:S(2)}, u32[]{:S(2)}) collective-permute-start(bf16[8,128,128]{2,1,0:T(8,128)(2,1)S(1)} %get-tuple-element.22), channel_id=1, source_target_pairs={{0,6},{2,4},{4,2},{6,0},{1,7},{3,5},{5,3},{7,1},{8,14},{10,12},{12... | collective-permute-start | bytes 786440 | tf_op jit(solution)/shard_map/projection_grad/ppermute | solution.py:22
  49.6 19.5 %collective-permute-start.2 = (bf16[8,128,128]{2,1,0:T(8,128)(2,1)S(1)}, bf16[8,128,128]{2,1,0:T(8,128)(2,1)S(1)}, u32[]{:S(2)}, u32[]{:S(2)}) collective-permute-start(bf16[8,128,128]{2,1,0:T(8,128)(2,1)S(1)} %get-tuple-element.23), channel_id=1, source_target_pairs={{0,2},{2,0},{4,6},{6,4},{1,3},{3,1},{5,7},{7,5},{8,10},{10,8},{12,... | collective-permute-start | bytes 786440 | tf_op jit(solution)/shard_map/projection_grad/ppermute | solution.py:22
  51.8 17.4 %collective-permute-start.3 = (bf16[8,128,128]{2,1,0:T(8,128)(2,1)S(1)}, bf16[8,128,128]{2,1,0:T(8,128)(2,1)S(1)}, u32[]{:S(2)}, u32[]{:S(2)}) collective-permute-start(bf16[8,128,128]{2,1,0:T(8,128)(2,1)S(1)} %get-tuple-element.24), channel_id=1, source_target_pairs={{0,4},{2,6},{4,0},{6,2},{1,5},{3,7},{5,1},{7,3},{8,12},{10,14},{12... | collective-permute-start | bytes 786440 | tf_op jit(solution)/shard_map/projection_grad/ppermute | solution.py:22
  53.8 6.0 %collective-permute-start.4 = (f32[64,448]{1,0:T(8,128)S(1)}, f32[64,448]{1,0:T(8,128)S(1)}, u32[]{:S(2)}, u32[]{:S(2)}) collective-permute-start(f32[64,448]{1,0:T(8,128)S(1)} %fusion.1), channel_id=1, source_target_pairs={{0,64},{64,0},{128,192},{192,128},{256,320},{320,256},{384,448},{4... | collective-permute-start | bytes 344072 | tf_op jit(solution)/shard_map/deltas_over_islands/ppermute | solution.py:22
  59.8 10.3 %collective-permute-start.5 = (f32[64,448]{1,0:T(8,128)S(1)}, f32[64,448]{1,0:T(8,128)}, u32[]{:S(2)}, u32[]{:S(2)}) collective-permute-start(f32[64,448]{1,0:T(8,128)S(1)} %add.31), channel_id=1, source_target_pairs={{0,192},{64,128},{128,64},{192,0},{256,448},{320,384},{384,320},{4... | collective-permute-start | bytes 344072 | tf_op jit(solution)/shard_map/deltas_over_islands/ppermute | solution.py:22
  64.5 22.0 %collective-permute-start.6 = (bf16[16,128,128]{2,1,0:T(8,128)(2,1)S(1)}, bf16[16,128,128]{2,1,0:T(8,128)(2,1)S(1)}, u32[]{:S(2)}, u32[]{:S(2)}) collective-permute-start(bf16[16,128,128]{2,1,0:T(8,128)(2,1)S(1)} %all-to-all-done.weight.w00), channel_id=1, source_target_pairs={{0,2},{2,0},{1,3},{3,1},{4,6},{6,4},{5,7},{7,5},{8,10},{10,8},{9,1... | collective-permute-start | bytes 1572872 | tf_op jit(solution)/shard_map/values/ppermute | solution.py:22
  70.1 39.3 %copy-start.5 = (f32[64,448]{1,0:T(8,128)S(1)}, f32[64,448]{1,0:T(8,128)}, u32[]{:S(2)}) copy-start(f32[64,448]{1,0:T(8,128)} %param.11) | copy-start | bytes 344068
  70.1 39.3 %copy-start.6 = (f32[64,448]{1,0:T(8,128)S(1)}, f32[64,448]{1,0:T(8,128)}, u32[]{:S(2)}) copy-start(f32[64,448]{1,0:T(8,128)} %param.13) | copy-start | bytes 344068
  70.1 29.6 %all-to-all-start.1 = ((bf16[8,144,128]{2,1,0:T(8,128)(2,1)}), bf16[8,144,128]{2,1,0:T(8,128)(2,1)S(1)}, u32[]{:S(2)}, u32[]{:S(2)}) async-start(bf16[8,144,128]{2,1,0:T(8,128)(2,1)} %combine.1), calls=%async_computation.1 | async-start | bytes 589824 | tf_op jit(solution)/shard_map/projection_grad/all_to_all | solution.py:214
  81.7 9.9 %collective-permute-start.7 = (bf16[16,128,128]{2,1,0:T(8,128)(2,1)S(1)}, bf16[16,128,128]{2,1,0:T(8,128)(2,1)S(1)}, u32[]{:S(2)}, u32[]{:S(2)}) collective-permute-start(bf16[16,128,128]{2,1,0:T(8,128)(2,1)S(1)} %all-to-all-done.weight.w00), channel_id=1, source_target_pairs={{0,1},{1,0},{2,3},{3,2},{4,5},{5,4},{6,7},{7,6},{8,9},{9,8},{10,11... | collective-permute-start | bytes 1572872 | tf_op jit(solution)/shard_map/values/ppermute | solution.py:22
  86.5 5.1 %collective-permute-start.8 = (bf16[16,128,128]{2,1,0:T(8,128)(2,1)S(1)}, bf16[16,128,128]{2,1,0:T(8,128)(2,1)S(1)}, u32[]{:S(2)}, u32[]{:S(2)}) collective-permute-start(bf16[16,128,128]{2,1,0:T(8,128)(2,1)S(1)} %collective-permute-done.6.w01), channel_id=1, source_target_pairs={{0,1},{1,0},{2,3},{3,2},{4,5},{5,4},{6,7},{7,6},{8,9},{9,8},{10,11... | collective-permute-start | bytes 1572872 | tf_op jit(solution)/shard_map/values/ppermute | solution.py:22
  89.4 20.0 %collective-permute-start.9 = (f32[64,448]{1,0:T(8,128)S(1)}, f32[64,448]{1,0:T(8,128)S(1)}, u32[]{:S(2)}, u32[]{:S(2)}) collective-permute-start(f32[64,448]{1,0:T(8,128)S(1)} %add.37), channel_id=1, source_target_pairs={{0,256},{64,320},{128,384},{192,448},{256,0},{320,64},{384,128},{4... | collective-permute-start | bytes 344072 | tf_op jit(solution)/shard_map/deltas_over_islands/ppermute | solution.py:22
  91.6 2.2 %copy-start.1 = (bf16[256,8192]{1,0:T(8,128)(2,1)S(1)}, bf16[256,8192]{1,0:T(8,128)(2,1)}, u32[]{:S(2)}) copy-start(bf16[256,8192]{1,0:T(8,128)(2,1)} %x.3) | copy-start | bytes 12582916
  100.3 14.6 %all-to-all-start.2 = ((f32[8,8,128]{2,1,0:T(8,128)}), f32[8,8,128]{2,1,0:T(8,128)S(1)}, u32[]{:S(2)}, u32[]{:S(2)}) async-start(f32[8,8,128]{2,1,0:T(8,128)} %broadcast_in_dim.10), calls=%async_computation.2 | async-start | bytes 65536 | tf_op jit(solution)/shard_map/gain_grad/all_to_all | solution.py:26
